TPU v7x, 32 devices: a whole 2x2x4 slice. The times are simulated.
32 devices in a mesh: groups: 2 (over y), seq: 4 (over z), dp: 4 (over x, core).
Axes of the slice: x: 2, y: 2, z: 4, core: 2. Of those that a mesh axis runs over, the one named last changes fastest.
Arguments:
- x_raw: bfloat16 [1024, 8192], P(('groups', 'seq'), 'dp'), parts along dimension 0, may hold values from -6 to 6
- bc_raw: bfloat16 [1024, 2048], P(('groups', 'seq'), 'dp'), parts along dimension 0, may hold values from -6 to 6
- z_gate: bfloat16 [1024, 8192], P(('groups', 'seq'), 'dp'), parts along dimension 0, may hold values from -6 to 6
- dt_raw: float32 [1024, 128], P(('groups', 'seq'), 'dp'), parts along dimension 0, may hold values from -3 to 6
- conv_x_weight: float32 [4, 8192], P(None, 'dp'), may hold values from -3 to 3
- conv_x_bias: float32 [8192], P('dp'), may hold values from -3 to 3
- conv_bc_weight: float32 [4, 2048], P(None, 'dp'), may hold values from -3 to 3
- conv_bc_bias: float32 [2048], P('dp'), may hold values from -3 to 3
- dt_bias: float32 [128], P('dp'), may hold values from -1 to 1
- a_log: float32 [128], P('dp')
- skip_d: float32 [128], P('dp'), may hold values from 0.5 to 1.5
- norm_gain: float32 [8192], P('dp'), may hold values from 0.5 to 1.5
- queries: bfloat16 [1024, 4096], P(('groups', 'seq'), 'dp'), parts along dimension 0, may hold values from -6 to 6
- keys: bfloat16 [1024, 1024], P(('groups', 'seq'), 'dp'), parts along dimension 0, may hold values from -6 to 6
- values: bfloat16 [1024, 1024], P(('groups', 'seq'), 'dp'), parts along dimension 0, may hold values from -6 to 6
- doc_lens: int32 [8], P('groups'), parts along dimension 0, may hold values from 1 to 256, 512 in all
Outputs:
- mamba_out: bfloat16 [1024, 8192], P(('groups', 'seq'), 'dp'), parts along dimension 0
- attn_out: bfloat16 [1024, 4096], P(('groups', 'seq'), 'dp'), parts along dimension 0
There are 2 independent parts, one for each index of `groups`. A program takes and returns all parts, laid end to end along the dimension named above; an argument that names none is the same for every part. Nothing has to cross between parts.
Inputs may be any that keep to these rules, and one draw needn't show every extreme that they name: doc_lens holds 4 document lengths that sum to 512; the longest is exactly 256.
All inputs are finite; a program needn't handle non-finite values.
Results may differ from a plain program's by a relative error of at most 0.018.
Values may be sent and summed in bfloat16 or wider, within the bound.
No kernel may reach another device: no remote copies, remote signals or barrier semaphores. Data moves between devices by JAX's collectives and lax.ppermute only.
A program may use at most 128 MiB of HBM per device.

v0:
```python
import functools
import math
from typing import NamedTuple

import jax
import jax.numpy as jnp
from jax import lax
from jax.experimental import pallas as pl
from jax.experimental.pallas import tpu as pltpu
from jax.sharding import PartitionSpec as P

HDIM = 64
STATE = 128
QHEADS = 32
KVHEADS = 8
ADIM = 128
EPSILON = 1e-05
BARRED = -2e30
HIGHEST = lax.Precision.HIGHEST
F32 = jnp.float32
BF16 = jnp.bfloat16
CHUNK = 256
EDGE = 16
KERNEL_FLOPS = 2 * 10**9
VMEM_LIMIT = 40 * 1024 * 1024
VMEM_ALL = 62 * 1024 * 1024


def silu(value):
    return value * (0.5 * jnp.tanh(0.5 * value) + 0.5)


def softplus(value):
    return jnp.maximum(value, 0.0) + jnp.log(1.0 + jnp.exp(-jnp.abs(value)))


def doc_start(positions, lens_ref):
    begin = jnp.int32(0)
    found = positions * 0
    for doc in range(lens_ref.shape[0]):
        found = jnp.where(positions >= begin, begin, found)
        begin = begin + lens_ref[doc]
    return found


def halves(value):
    high = value.astype(BF16)
    return high, (value - high.astype(F32)).astype(BF16)


def widen(per_head, first, width):
    heads = per_head.shape[1]
    both = jnp.concatenate(halves(per_head), axis=1)
    head = lax.broadcasted_iota(jnp.int32, (2 * heads, width), 0)
    head = jnp.where(head >= heads, head - heads, head)
    channel = lax.broadcasted_iota(jnp.int32, (2 * heads, width), 1) + first
    spread = (channel // HDIM == head).astype(F32).astype(BF16)
    return jnp.dot(both, spread, preferred_element_type=F32)


def rates(dt_ref, dt_bias_ref, a_log_ref):
    heads = dt_ref.shape[0]
    step = softplus(dt_ref[...].T + dt_bias_ref[...].reshape(1, -1)[:, :heads])
    rate = -step * jnp.exp(a_log_ref[...].reshape(1, -1)[:, :heads])
    rows = step.shape[0]
    row = lax.broadcasted_iota(jnp.int32, (rows, rows), 0)
    column = lax.broadcasted_iota(jnp.int32, (rows, rows), 1)
    lower = (row >= column).astype(F32).astype(BF16)
    high = rate.astype(BF16)
    middle, low = halves(rate - high.astype(F32))
    parts = jnp.concatenate([high, middle, low], axis=0)
    lowers = jnp.concatenate([lower, lower, lower], axis=1)
    return step, jnp.dot(lowers, parts, preferred_element_type=F32)


def insides(first, shape, taps, lens_ref):
    positions = first + lax.broadcasted_iota(jnp.int32, shape, 0)
    depth = positions - doc_start(positions, lens_ref)
    return [depth >= lag for lag in range(taps)]


def conv(pad, rows, weight, bias, inside):
    taps = weight.shape[0]
    total = pad[8 : 8 + rows] * weight[taps - 1 : taps] + bias
    for lag in range(1, taps):
        term = pad[8 - lag : 8 - lag + rows] * weight[taps - 1 - lag : taps - lag]
        total = total + jnp.where(inside[lag], term, 0.0)
    return silu(total)


def tail_lines(message, rows):
    block = message[rows:].astype(F32)
    return jnp.concatenate([block[at : at + 4] for at in range(0, block.shape[0], 4)], axis=1)


def reach(device, rows, lens_ref):
    return device - doc_start((device + 1) * rows - 1, lens_ref) // rows


def kept_weight(here, step, running, taps, lens_ref):
    rows = step.shape[0]
    last_begin = doc_start((here + 1) * rows - 1, lens_ref)
    row = lax.broadcasted_iota(jnp.int32, step.shape, 0)
    weight = step * jnp.exp(running[rows - 1 : rows] - running)
    kept = (here * rows + row >= last_begin) & ((row >= taps - 1) | (last_begin // rows >= here))
    return jnp.where(kept, weight, 0.0)


def conv_rows(pad, raw, weight, bias, inside):
    pad[0:8] = jnp.zeros((8, raw.shape[1]), F32)
    pad[8:] = raw.astype(F32)
    return conv(pad, raw.shape[0], weight, bias.reshape(1, -1), inside)


def first_state_kernel(*refs):
    hbm_refs, out_hbm_ref = refs[:10], refs[10]
    vmem_refs = refs[11:21]
    x_edge_ref, bc_edge_ref, out_ref, b_pad_ref, pad_ref, in_sems, out_sems = refs[21:]
    x_ref, b_ref, dt_ref, wx_ref, bx_ref, wbc_ref, bbc_ref, dt_bias_ref, a_log_ref, lens_ref = vmem_refs
    rows, width = x_ref.shape
    taps = wx_ref.shape[0]

    def corner(ref, shape):
        return ref.at[tuple(pl.ds(0, extent) for extent in shape)]

    order = (0, 9, 2, 7, 8, 1, 5, 6, 3, 4)
    copies = {}
    for at in order:
        source = corner(hbm_refs[at], vmem_refs[at].shape)
        copies[at] = pltpu.make_async_copy(source, vmem_refs[at], in_sems.at[at])
        copies[at].start()
    edge_copies = []
    for at, (source, target) in enumerate(((hbm_refs[0], x_edge_ref), (hbm_refs[1], bc_edge_ref))):
        edge_copies.append(
            pltpu.make_async_copy(source.at[pl.ds(rows - EDGE, EDGE)], target, in_sems.at[10 + at])
        )
        edge_copies[-1].start()

    here = lax.axis_index("seq")
    for at in (9, 2, 7, 8):
        copies[at].wait()
    inside = insides(here * rows, (rows, CHUNK), taps, lens_ref)
    step, running = rates(dt_ref, dt_bias_ref, a_log_ref)
    weight = kept_weight(here, step, running, taps, lens_ref)
    narrow = [mask[:, :STATE] for mask in inside]
    for at in (1, 5, 6):
        copies[at].wait()
    inputs = conv_rows(b_pad_ref, b_ref[...], wbc_ref[...], bbc_ref[...], narrow)
    turned = inputs.T.astype(BF16)
    for at in (0, 3, 4):
        copies[at].wait()
    slots = pad_ref.shape[0]
    outs = []

    def send(at, view):
        copy = pltpu.make_async_copy(out_ref.at[view], out_hbm_ref.at[view], out_sems.at[at])
        copy.start()
        outs.append(copy)

    for at, start in enumerate(range(0, width, CHUNK)):
        columns = slice(start, start + CHUNK)
        pad = pad_ref.at[(at + 1) % slots]
        xc = conv_rows(pad, x_ref[:, columns], wx_ref[:, columns], bx_ref[:, columns], inside)
        weighted = (xc * widen(weight, start, CHUNK)).astype(BF16)
        out_ref[:STATE, columns] = jnp.dot(turned, weighted, preferred_element_type=F32).astype(BF16)
        if at % 2:
            send(at // 2, (pl.ds(0, STATE), pl.ds(start - CHUNK, 2 * CHUNK)))
    for copy in edge_copies:
        copy.wait()
    edges = jnp.concatenate([x_edge_ref[...].astype(F32), bc_edge_ref[...].astype(F32)], axis=1)[EDGE - 4 :]
    spare = -edges.shape[1] % width
    if spare:
        edges = jnp.concatenate([edges, jnp.zeros((4, spare), F32)], axis=1)
    pieces = [edges[:, at : at + width] for at in range(0, edges.shape[1], width)]
    while len(pieces) % (EDGE // 4):
        pieces.append(jnp.zeros_like(pieces[0]))
    out_ref[STATE:] = jnp.concatenate(pieces, axis=0).astype(BF16)
    send(width // (2 * CHUNK), (pl.ds(STATE, out_ref.shape[0] - STATE), pl.ds(0, width)))
    for copy in outs:
        copy.wait()


def prepare_kernel(hops, groups, *refs):
    x_ref, bc_ref, dt_ref, wx_ref, bx_ref, wbc_ref, bbc_ref, dt_bias_ref, a_log_ref, skip_ref, lens_ref = refs[:11]
    z_ref = refs[11]
    xc_ref, bcc_ref, partial_ref, weight_ref, through_ref, inside_ref, flag_ref = refs[12:19]
    wide_skip_ref, begin_ref, step_ref, running_ref, out_ref, gate_ref, decay_ref = refs[19:26]
    state_refs = refs[26:-2]
    top_ref, pad_ref = refs[-2:]
    rows, width = x_ref.shape
    per_group = width // groups
    taps = wx_ref.shape[0]
    slots = pad_ref.shape[0]
    here = lax.axis_index("seq")
    first = here * rows
    inside = insides(first, (rows, CHUNK), taps, lens_ref)
    step, running = rates(dt_ref, dt_bias_ref, a_log_ref)
    heads = step.shape[1]
    group_heads = heads // groups
    kept = kept_weight(here, step, running, taps, lens_ref)
    for group in range(groups):
        base = slice(group * 2 * STATE, (group + 1) * 2 * STATE)
        pair = conv_rows(pad_ref.at[0], bc_ref[:, base], wbc_ref[:, base], bbc_ref[base], inside)
        bcc_ref[:, base] = pair.astype(BF16)
        turned = pair[:, :STATE].T.astype(BF16)
        part_weight = kept[:, group * group_heads : (group + 1) * group_heads]
        for chunk in range(0, per_group, CHUNK):
            columns = slice(group * per_group + chunk, group * per_group + chunk + CHUNK)
            pad = pad_ref.at[(chunk // CHUNK + 1) % slots]
            xc = conv_rows(pad, x_ref[:, columns], wx_ref[:, columns], bx_ref[columns], inside)
            xc_ref[:, columns] = xc.astype(BF16)
            if group:
                weighted = (xc * widen(part_weight, chunk, CHUNK)).astype(BF16)
                state_refs[group - 1][:, chunk : chunk + CHUNK] = jnp.dot(
                    turned, weighted, preferred_element_type=F32
                ).astype(BF16)

    own = reach(here, rows, lens_ref) == 0
    inside = [mask[:8] for mask in inside]
    for lag in range(1, taps):
        inside_ref[lag - 1] = inside[lag].astype(F32)
    flag_ref[0] = jnp.broadcast_to(own.astype(F32), (8, CHUNK))
    before = reach(here - 1, rows, lens_ref)
    for hop in range(1, hops):
        flag_ref[hop] = jnp.broadcast_to((before == hop).astype(F32), (8, CHUNK))
    begin = doc_start(first + lax.broadcasted_iota(jnp.int32, begin_ref.shape, 0), lens_ref)
    begin_ref[...] = begin
    entry = jnp.where(begin[:, :heads] < first, jnp.exp(running), 0.0)
    step_ref[...] = step
    running_ref[...] = running
    row = lax.broadcasted_iota(jnp.int32, (8, heads), 0)
    total = running[rows - 1 : rows]
    weight = step[:8] * jnp.exp(total - running[:8])
    weight = jnp.where((row < taps - 1) & jnp.logical_not(own), weight, 0.0)
    through = jnp.where(own, 0.0, jnp.broadcast_to(jnp.exp(total), (8, heads)))
    skip = jnp.broadcast_to(skip_ref[...].reshape(1, -1), (8, heads))
    every = jnp.concatenate([weight, through, skip], axis=0)
    for start in range(0, width, CHUNK):
        wide = widen(every, start, CHUNK)
        weight_ref[:, start : start + CHUNK] = wide[:8]
        through_ref[:, start : start + CHUNK] = wide[8:16]
        wide_skip_ref[:, start : start + CHUNK] = wide[16:]
    top_ref[0:8] = jnp.zeros((8, top_ref.shape[1]), F32)
    top_ref[8:, :width] = x_ref[:EDGE].astype(F32)[:8]
    top_ref[8:, width:] = bc_ref[:EDGE].astype(F32)[:8]

    def some(columns, base, w_ref, b_ref):
        here_columns = slice(base + columns.start, base + columns.stop)
        total = top_ref[8:, here_columns] * w_ref[taps - 1 : taps, columns] + b_ref[columns].reshape(1, -1)
        for lag in range(1, taps):
            term = top_ref[8 - lag : 16 - lag, here_columns] * w_ref[taps - 1 - lag : taps - lag, columns]
            total = total + jnp.where(inside[lag], term, 0.0)
        partial_ref[:, here_columns] = total

    for start in range(0, width, CHUNK):
        some(slice(start, start + CHUNK), 0, wx_ref, bx_ref)
    for start in range(0, bc_ref.shape[1], CHUNK):
        some(slice(start, start + CHUNK), width, wbc_ref, bbc_ref)

    row = lax.broadcasted_iota(jnp.int32, (rows, rows), 0)
    lane = lax.broadcasted_iota(jnp.int32, (rows, rows), 1)
    linked = (row >= lane) & (first + lane >= begin) & (lane >= 8)
    turned_running = running.T
    turned_step = step.T
    pair_width = 2 * HDIM
    channel = lax.broadcasted_iota(jnp.int32, (rows, pair_width), 1)
    below = lax.broadcasted_iota(jnp.int32, (rows, CHUNK), 0) >= 8
    for group in range(groups):
        base = group * 2 * STATE
        meet = lax.dot_general(
            bcc_ref[:, base + STATE : base + 2 * STATE],
            bcc_ref[:, base : base + STATE],
            (((1,), (1,)), ((), ())),
            preferred_element_type=F32,
        )
        meet = jnp.where(linked, meet, 0.0)
        group_entry = entry[:, group * group_heads : (group + 1) * group_heads]
        for chunk in range(0, per_group, CHUNK):
            at = group * per_group + chunk
            columns = slice(at, at + CHUNK)
            gate = silu(z_ref[:, columns].astype(F32))
            gate_ref[:, columns] = gate
            decay_ref[:, columns] = widen(group_entry, chunk, CHUNK) * gate
            xc_all = xc_ref[:, columns]
            skipped = jnp.where(below, xc_all.astype(F32) * wide_skip_ref[0:1, columns], 0.0)
            for start in range(0, CHUNK, pair_width):
                parts = []
                for head in ((at + start) // HDIM, (at + start) // HDIM + 1):
                    spread = running[:, head : head + 1] - turned_running[head : head + 1]
                    decay = jnp.exp(jnp.minimum(spread, 0.0))
                    parts.append((decay * (meet * turned_step[head : head + 1])).astype(BF16))
                mix = jnp.concatenate(parts, axis=1)
                here_columns = slice(start, start + pair_width)
                xc = xc_all[:, here_columns]
                zero = jnp.zeros_like(xc)
                stacked = jnp.concatenate(
                    [jnp.where(channel < HDIM, xc, zero), jnp.where(channel < HDIM, zero, xc)], axis=0
                )
                value = jnp.dot(mix, stacked, preferred_element_type=F32) + skipped[:, here_columns]
                out_ref[:, at + start : at + start + pair_width] = value * gate[:, here_columns]


def first_rows(lines, partial_ref, inside_ref, w_ref, pad_ref, slot, at, start):
    taps = w_ref.shape[0]
    columns = slice(start, start + CHUNK)
    pad = pad_ref.at[slot]
    pad[4:8] = lines[:, at + start : at + start + CHUNK]
    pad[8:] = jnp.zeros((8, CHUNK), F32)
    total = partial_ref[:, at + start : at + start + CHUNK]
    for lag in range(1, taps):
        term = pad[8 - lag : 16 - lag] * w_ref[taps - 1 - lag : taps - lag, columns]
        total = total + term * inside_ref[lag - 1]
    return silu(total)


def sixteen(value):
    return jnp.concatenate([value, jnp.zeros_like(value)], axis=0).astype(BF16)


def relay_first_kernel(fresh, *refs):
    message_ref, state_ref, partial_ref, weight_ref, through_ref, inside_ref, flag_ref, wx_ref, wbc_ref = refs[:9]
    other_ref = refs[9] if fresh else state_ref
    out_ref, pad_ref = refs[-2:]
    width = out_ref.shape[1]
    slots = pad_ref.shape[0]
    lines = tail_lines(message_ref, STATE)
    top = functools.partial(first_rows, lines, partial_ref, inside_ref)
    inputs = top(wbc_ref, pad_ref, 0, wx_ref.shape[1], 0)[:, :STATE]
    turned = jnp.concatenate([inputs, inputs], axis=0).T.astype(BF16)
    own = flag_ref[0, 0:1] > 0.5
    for start in range(0, width, CHUNK):
        columns = slice(start, start + CHUNK)
        xc = top(wx_ref, pad_ref, (start // CHUNK + 1) % slots, 0, start)
        weighted = sixteen(xc * weight_ref[:, columns])
        full = state_ref[:STATE, columns].astype(F32) + jnp.dot(
            turned, weighted, preferred_element_type=F32
        )
        full = full + through_ref[0:1, columns] * message_ref[:STATE, columns].astype(F32)
        out_ref[:, columns] = jnp.where(own, other_ref[:STATE, columns].astype(F32), full).astype(BF16)


def relay_kernel(part, fresh, *refs):
    got_ref, state_ref, through_ref, flag_ref = refs[:4]
    out_ref = refs[-1]
    width = out_ref.shape[1]
    own = flag_ref[0, 0:1] > 0.5
    for start in range(0, width, CHUNK):
        columns = slice(start, start + CHUNK)
        through = through_ref[0:1, part * width + start : part * width + start + CHUNK]
        full = state_ref[:, columns].astype(F32) + through * got_ref[:STATE, columns].astype(F32)
        if fresh:
            full = jnp.where(own, refs[4][:STATE, columns].astype(F32), full)
        out_ref[:, columns] = full.astype(BF16)


def first_rows_kernel(groups, *refs):
    (
        message_ref, partial_ref, weight_ref, inside_ref, wx_ref, wbc_ref, step_ref, running_ref,
        wide_skip_ref, begin_ref, bcc_ref, main_ref, gate_ref,
    ) = refs[:13]
    state_refs = refs[13 : 13 + groups]
    out_ref, c_ref = refs[13 + groups : 15 + groups]
    full_refs = refs[15 + groups : 15 + 2 * groups]
    pad_ref = refs[-1]
    rows, width = main_ref.shape
    per_group = width // groups
    heads = per_group // HDIM
    lanes = 8 * heads
    first = lax.axis_index("seq") * rows
    lines = tail_lines(message_ref, STATE)
    slots = pad_ref.shape[0]
    top = functools.partial(first_rows, lines, partial_ref, inside_ref)
    lane = lax.broadcasted_iota(jnp.int32, (rows, lanes), 1)
    line = lane & 7
    row = lax.broadcasted_iota(jnp.int32, (rows, lanes), 0)
    begin = jnp.concatenate([begin_ref[...]] * -(-lanes // rows), axis=1)[:, :lanes]
    linked = (row >= line) & (first + line >= begin)
    head = lax.broadcasted_iota(jnp.int32, (3 * heads, lanes), 0)
    for _ in range(2):
        head = jnp.where(head >= heads, head - heads, head)
    spread = (lax.broadcasted_iota(jnp.int32, (3 * heads, lanes), 1) >> 3 == head).astype(F32).astype(BF16)
    own_line = lax.broadcasted_iota(jnp.int32, (8, lanes), 0) == line[:8]

    def to_lanes(value):
        high = value.astype(BF16)
        middle, low = halves(value - high.astype(F32))
        return jnp.dot(jnp.concatenate([high, middle, low], axis=1), spread, preferred_element_type=F32)

    def by_line(value):
        return jnp.sum(jnp.where(own_line, value, 0.0), axis=0, keepdims=True)

    channel = lax.broadcasted_iota(jnp.int32, (8, CHUNK), 1)
    for group in range(groups):
        base = group * 2 * STATE
        these = slice(group * heads, (group + 1) * heads)
        new = top(wbc_ref, pad_ref, group % slots, width, base)
        old = bcc_ref[:, base + STATE : base + 2 * STATE]
        outputs = jnp.concatenate([new[:, STATE:], old[:EDGE].astype(F32)[8:]], axis=0).astype(BF16)
        outputs = jnp.concatenate([outputs, old[EDGE:]], axis=0)
        c_ref[:, group * STATE : (group + 1) * STATE] = outputs
        inputs = jnp.concatenate([new[:, :STATE]] * heads, axis=0).astype(BF16)
        meet = lax.dot_general(
            outputs, inputs, (((1,), (1,)), ((), ())), preferred_element_type=F32
        )
        running = to_lanes(running_ref[:, these])
        decay = jnp.exp(jnp.minimum(running - by_line(running[:8]), 0.0))
        mix = decay * (meet * by_line(to_lanes(step_ref[:8, these])))
        mix = jnp.where(linked, mix, 0.0).astype(BF16)
        turned = inputs[:EDGE].astype(F32).T.astype(BF16)
        for chunk in range(0, per_group, CHUNK):
            at = group * per_group + chunk
            columns = slice(at, at + CHUNK)
            xc = top(wx_ref, pad_ref, (chunk // CHUNK + 1) % slots, 0, at)
            full = state_refs[group][:STATE, chunk : chunk + CHUNK].astype(F32) + jnp.dot(
                turned, sixteen(xc * weight_ref[:, columns]), preferred_element_type=F32
            )
            full_refs[group][:, chunk : chunk + CHUNK] = full.astype(BF16)
            blocks = []
            for at_head in range(heads):
                low = at_head * HDIM - chunk
                if 0 <= low < CHUNK:
                    blocks.append(jnp.where((channel >= low) & (channel < low + HDIM), xc, 0.0))
                else:
                    blocks.append(jnp.zeros_like(xc))
            spread_xc = jnp.concatenate(blocks, axis=0).astype(BF16)
            gate = gate_ref[:, columns]
            value = main_ref[:, columns] + gate * jnp.dot(mix, spread_xc, preferred_element_type=F32)
            out_ref[:, columns] = value
            out_ref[0:8, columns] = value[:8] + gate[:8] * (xc * wide_skip_ref[:, columns])


def attend(q_ref, kv_refs, begin_ref, blocks, share, head):
    rows = q_ref.shape[0]
    kv_heads = kv_refs[0].shape[1] // (2 * ADIM)
    count = rows * blocks.count
    here = lax.axis_index("seq")
    row = here * rows + lax.broadcasted_iota(jnp.int32, (rows, count), 0)
    lane = (here - blocks.farthest) * rows + lax.broadcasted_iota(jnp.int32, (rows, count), 1)
    begin = jnp.concatenate([begin_ref[...]] * blocks.count, axis=1)
    allowed = jnp.concatenate([(lane <= row) & (lane >= begin)] * share, axis=0)
    low = head * ADIM
    keys = jnp.concatenate([ref[:, low : low + ADIM] for ref in kv_refs], axis=0)
    low = (kv_heads + head) * ADIM
    values = jnp.concatenate([ref[:, low : low + ADIM] for ref in kv_refs], axis=0)
    values = jnp.concatenate([values, jnp.ones((count, ADIM), BF16)], axis=1)
    lows = [(head * share + part) * ADIM for part in range(share)]
    asking = jnp.concatenate([q_ref[:, low : low + ADIM] for low in lows], axis=0)
    scores = lax.dot_general(asking, keys, (((1,), (1,)), ((), ())), preferred_element_type=F32)
    return jnp.where(allowed, scores * ADIM ** (-0.5), BARRED), values


class Blocks(NamedTuple):
    farthest: int
    count: int


def fold(q_ref, kv_refs, begin_ref, blocks, share, head, carry):
    lows = [(head * share + part) * ADIM for part in range(share)]
    scores, values = attend(q_ref, kv_refs, begin_ref, blocks, share, head)
    peak = jnp.max(scores, axis=1, keepdims=True)
    peak = jnp.broadcast_to(peak, (peak.shape[0], ADIM))
    if carry is not None:
        sums, totals, before = (
            jnp.concatenate([ref[:, low : low + ADIM] for low in lows], axis=0) for ref in carry
        )
        peak = jnp.maximum(peak, before)
    expo = jnp.exp(scores - jnp.concatenate([peak] * (scores.shape[1] // ADIM), axis=1))
    summed = jnp.dot(expo.astype(BF16), values, preferred_element_type=F32)
    if carry is None:
        return lows, summed[:, :ADIM], summed[:, ADIM:], peak
    factor = jnp.exp(before - peak)
    return lows, sums * factor + summed[:, :ADIM], totals * factor + summed[:, ADIM:], peak


def own_kernel(q_ref, keys_ref, values_ref, begin_ref, *outs):
    kv_ref = outs[3]
    kv_width = keys_ref.shape[1]
    kv_ref[:, :kv_width] = keys_ref[...]
    kv_ref[:, kv_width:] = values_ref[...]
    rows = q_ref.shape[0]
    share = QHEADS // KVHEADS
    for head in range(kv_width // ADIM):
        lows, *results = fold(q_ref, (kv_ref,), begin_ref, Blocks(0, 1), share, head, None)
        for ref, result in zip(outs, results):
            for part, low in enumerate(lows):
                ref[:, low : low + ADIM] = result[part * rows : (part + 1) * rows]


def near_kernel(q_ref, before_ref, begin_ref, *refs):
    carry, outs = refs[:3], refs[4:]
    outs[3][...] = before_ref[...]
    rows = q_ref.shape[0]
    share = QHEADS // KVHEADS
    for head in range(before_ref.shape[1] // (2 * ADIM)):
        lows, *results = fold(q_ref, (before_ref,), begin_ref, Blocks(1, 1), share, head, carry)
        for ref, result in zip(outs, results):
            for part, low in enumerate(lows):
                ref[:, low : low + ADIM] = result[part * rows : (part + 1) * rows]


def far_kernel(hops, *refs):
    q_ref, begin_ref = refs[:2]
    kv_refs = refs[5 : 4 + hops]
    out_hbm_ref, out_ref, sems = refs[4 + hops :]
    rows = q_ref.shape[0]
    share = QHEADS // KVHEADS
    copies = []
    for head in range(kv_refs[0].shape[1] // (2 * ADIM)):
        blocks = Blocks(hops, hops - 1)
        lows, sums, totals, _ = fold(q_ref, kv_refs, begin_ref, blocks, share, head, refs[2:5])
        result = (sums / totals).astype(BF16)
        for part, low in enumerate(lows):
            out_ref[:, low : low + ADIM] = result[part * rows : (part + 1) * rows]
        columns = pl.ds(head * share * ADIM, share * ADIM)
        copies.append(
            pltpu.make_async_copy(out_ref.at[:, columns], out_hbm_ref.at[:, columns], sems.at[head])
        )
        copies[-1].start()
    for copy in copies:
        copy.wait()


def norm_kernel(part, hops, first, where, given, *refs):
    local_ref, decay_ref, c_ref, gain_ref, flag_ref = refs[:5]
    got_refs = refs[5 : 5 + hops]
    out_hbm_ref, *token_refs = refs[5 + hops + given : -3]
    gated_ref, out_ref, sems = refs[-3:]
    for ref in token_refs:
        ref[...] = jnp.zeros_like(ref)

    def work():
        rows, width = gated_ref.shape
        outputs = c_ref[:, part * STATE : (part + 1) * STATE]
        squares = jnp.zeros((rows, 128), F32)
        for start in range(0, width, CHUNK):
            columns = slice(start, start + CHUNK)
            placed = slice(part * width + start, part * width + start + CHUNK)
            state = got_refs[0][:STATE, columns]
            for hop in range(1, hops):
                there = flag_ref[first + hop, 0:1] > 0.5
                state = jnp.where(there, got_refs[hop][:STATE, columns].astype(F32), state.astype(F32))
            carried = jnp.dot(outputs, state.astype(BF16), preferred_element_type=F32)
            gated = local_ref[:, placed] + carried * decay_ref[:, placed]
            gated_ref[:, columns] = gated
            for lane in range(0, CHUNK, 128):
                squares = squares + gated[:, lane : lane + 128] * gated[:, lane : lane + 128]
        squares = jnp.sum(squares, axis=1, keepdims=True)
        multiplier = lax.rsqrt(squares * (1.0 / width) + EPSILON)
        copies = []
        for start in range(0, width, CHUNK):
            columns = slice(start, start + CHUNK)
            gain = gain_ref[part * width + start : part * width + start + CHUNK]
            out_ref[:, columns] = (gated_ref[:, columns] * multiplier * gain.reshape(1, -1)).astype(BF16)
            copies.append(
                pltpu.make_async_copy(
                    out_ref.at[:, pl.ds(start, CHUNK)],
                    out_hbm_ref.at[:, pl.ds(part * width + start, CHUNK)],
                    sems.at[start // CHUNK],
                )
            )
            copies[-1].start()
        for copy in copies:
            copy.wait()

    odd = lax.axis_index("dp") % 2 == 1
    later = sum(flag_ref[hop, 0, 0] for hop in range(1, flag_ref.shape[0])) > 0.5
    here = {"odd": odd, "rest": jnp.logical_not(odd) | later, "first": jnp.logical_not(later), "later": later}
    pl.when(here[where])(work)


WHOLE = pl.BlockSpec(memory_space=pltpu.VMEM)
SCALARS = pl.BlockSpec(memory_space=pltpu.SMEM)
UNTOUCHED = pl.BlockSpec(memory_space=pl.ANY)


def tile(rows, columns, row, column):
    return pl.BlockSpec((rows, columns), lambda step: (row, column))


def call(kernel, name, outs, operands, specs, out_specs=None, scratch=(), flops=KERNEL_FLOPS, aliases={}, limit=VMEM_LIMIT):
    moved = sum(math.prod(a.shape) * a.dtype.itemsize for a in (*operands, *outs))
    return pl.pallas_call(
        kernel,
        name=name,
        grid=(1,),
        out_shape=outs,
        in_specs=specs,
        out_specs=[WHOLE] * len(outs) if out_specs is None else out_specs,
        scratch_shapes=list(scratch),
        input_output_aliases=aliases,
        compiler_params=pltpu.CompilerParams(vmem_limit_bytes=limit),
        cost_estimate=pl.CostEstimate(flops=flops, bytes_accessed=moved, transcendentals=0),
    )(*operands)


def onward(value, first=0):
    count = lax.axis_size("seq")
    return lax.ppermute(value, "seq", [(source, source + 1) for source in range(first, count - 1)])


def shards(
    x_raw,
    bc_raw,
    z_gate,
    dt_raw,
    conv_x_weight,
    conv_x_bias,
    conv_bc_weight,
    conv_bc_bias,
    dt_bias,
    a_log,
    skip_d,
    norm_gain,
    queries,
    keys,
    values,
    doc_lens,
):
    rows, width = x_raw.shape
    bc_width = bc_raw.shape[1]
    heads = dt_raw.shape[1]
    groups = bc_width // (2 * STATE)
    per_group = width // groups
    count = lax.axis_size("seq")
    longest = rows * count // 2
    hops = min(count - 1, -(-(longest - 1) // rows))
    assert hops * rows >= longest and (hops == 2 or hops > 2 and groups == 1)
    shape = jax.ShapeDtypeStruct
    dt = dt_raw.T
    params = [dt, conv_x_weight, conv_x_bias, conv_bc_weight, conv_bc_bias, dt_bias, a_log]
    pieces = -(-(width + bc_width) // per_group)
    tail_rows = EDGE * -(-4 * pieces // EDGE)

    (message,) = call(
        first_state_kernel,
        "first_state",
        [shape((STATE + tail_rows, per_group), BF16)],
        [x_raw, bc_raw, *(a if a.ndim > 1 else a[None] for a in params), doc_lens],
        [UNTOUCHED] * 10,
        out_specs=[UNTOUCHED],
        scratch=[
            pltpu.VMEM((rows, per_group), BF16),
            pltpu.VMEM((rows, STATE), BF16),
            pltpu.VMEM((per_group // HDIM, rows), F32),
            pltpu.VMEM((conv_x_weight.shape[0], per_group), F32),
            pltpu.VMEM((1, per_group), F32),
            pltpu.VMEM((conv_x_weight.shape[0], STATE), F32),
            pltpu.VMEM((1, STATE), F32),
            pltpu.VMEM((1, heads), F32),
            pltpu.VMEM((1, heads), F32),
            pltpu.SMEM(doc_lens.shape, jnp.int32),
            pltpu.VMEM((EDGE, width), BF16),
            pltpu.VMEM((EDGE, bc_width), BF16),
            pltpu.VMEM((STATE + tail_rows, per_group), BF16),
            pltpu.VMEM((rows + 8, STATE), F32),
            pltpu.VMEM((4, rows + 8, CHUNK), F32),
            pltpu.SemaphoreType.DMA((12,)),
            pltpu.SemaphoreType.DMA((per_group // (2 * CHUNK) + 1,)),
        ],
        limit=VMEM_ALL,
    )
    slots = [onward(message)]
    prepared = call(
        functools.partial(prepare_kernel, hops, groups),
        "prepare",
        [
            shape((rows, width), BF16),
            shape((rows, bc_width), BF16),
            shape((8, width + bc_width), F32),
            shape((8, width), F32),
            shape((8, width), F32),
            shape((conv_x_weight.shape[0] - 1, 8, CHUNK), F32),
            shape((hops, 8, CHUNK), F32),
            shape((8, width), F32),
            shape((rows, rows), jnp.int32),
            shape((rows, heads), F32),
            shape((rows, heads), F32),
            shape((rows, width), F32),
            shape((rows, width), F32),
            shape((rows, width), F32),
            *(shape((STATE, per_group), BF16) for _ in range(groups - 1)),
        ],
        [x_raw, bc_raw, *params, skip_d, doc_lens, z_gate],
        [WHOLE] * 10 + [SCALARS] + [WHOLE],
        scratch=[
            pltpu.VMEM((16, width + bc_width), F32),
            pltpu.VMEM((4, rows + 8, CHUNK), F32),
        ],
    )
    _, bcc, partial, weight, through, inside, flags, wide_skip, begin, *prepared = prepared
    step, running, main, gate, decay, *states = prepared
    states = [message, *states]
    carried = [shape(queries.shape, F32)] * 3 + [shape((rows, 2 * keys.shape[1]), BF16)]
    *carry, kv = call(own_kernel, "attend_own", carried, [queries, keys, values, begin], [WHOLE] * 4)
    kvs = [kv, onward(kv)]
    fulls = None
    for slot in range(2, hops + groups):
        part = min(slot - 1, groups) - 1
        fresh = slot <= groups
        if slot == 2:
            kernel = functools.partial(relay_first_kernel, fresh)
            operands = [slots[0], states[0], partial, weight, through, inside, flags, conv_x_weight, conv_bc_weight]
            scratch = [pltpu.VMEM((4, 16, CHUNK), F32)]
        else:
            kernel = functools.partial(relay_kernel, part, fresh)
            operands = [slots[-1], fulls[part], through, flags]
            scratch = []
        if fresh:
            operands.append(states[slot - 1])
        (passed,) = call(
            kernel,
            f"relay_slot{slot}",
            [shape((STATE, per_group), BF16)],
            operands,
            [WHOLE] * len(operands),
            scratch=scratch,
        )
        slots.append(onward(passed, max(0, slot - groups)))
        if fulls is None:
            gated, c_out, *fulls = call(
                functools.partial(first_rows_kernel, groups),
                "first_rows",
                [
                    shape((rows, width), F32),
                    shape((rows, groups * STATE), BF16),
                    *(shape((STATE, per_group), BF16) for _ in range(groups)),
                ],
                [
                    slots[0], partial, weight, inside, conv_x_weight, conv_bc_weight, step, running,
                    wide_skip, begin, bcc, main, gate, *states,
                ],
                [WHOLE] * (13 + groups),
                scratch=[pltpu.VMEM((4, 16, CHUNK), F32)],
            )
    def norm(part, first, stop, where, out=None, token=False):
        got = slots[part + first : part + stop]
        operands = [gated, decay, c_out, norm_gain, flags, *got]
        specs = [WHOLE] * len(operands)
        outs = [shape((rows, width), BF16)] + [shape((8, 128), F32)] * token
        aliases = {}
        if out is not None:
            aliases = {len(operands): 0}
            operands.append(out)
            specs.append(UNTOUCHED)
        return call(
            functools.partial(norm_kernel, part, len(got), first, where, out is not None),
            f"norm_part{part}_{where}",
            outs,
            operands,
            specs,
            out_specs=[UNTOUCHED] + [WHOLE] * token,
            scratch=[
                pltpu.VMEM((rows, per_group), F32),
                pltpu.VMEM((rows, per_group), BF16),
                pltpu.SemaphoreType.DMA((per_group // CHUNK,)),
            ],
            aliases=aliases,
            flops=KERNEL_FLOPS // 2,
        )

    mamba_out, token = None, c_out
    for part in range(groups - 1):
        mamba_out, token = norm(part, 0, 1, "odd", mamba_out, True)
    *carry, kv_on = call(
        near_kernel,
        "attend_near",
        carried,
        [queries, kvs[1], begin, *carry, token],
        [WHOLE] * 6 + [UNTOUCHED],
    )
    for hop in range(1, hops):
        kvs.append(onward(kv_on if hop == 1 else kvs[-1], hop))
    (attn_out,) = call(
        functools.partial(far_kernel, hops),
        "attend_far",
        [shape(queries.shape, BF16)],
        [queries, begin, *carry, *reversed(kvs[2:])],
        [WHOLE] * (4 + hops),
        out_specs=[UNTOUCHED],
        scratch=[
            pltpu.VMEM(queries.shape, BF16),
            pltpu.SemaphoreType.DMA((keys.shape[1] // ADIM,)),
        ],
    )
    for part in range(groups - 1):
        (mamba_out,) = norm(part, 0, hops, "rest", mamba_out)
    (mamba_out,) = norm(groups - 1, 0, 1, "first", mamba_out)
    (mamba_out,) = norm(groups - 1, 1, hops, "later", mamba_out)
    return (mamba_out, attn_out)


def solution(mesh):
    split = P(("groups", "seq"), "dp")
    placed = (
        split,
        split,
        split,
        split,
        P(None, "dp"),
        P("dp"),
        P(None, "dp"),
        P("dp"),
        P("dp"),
        P("dp"),
        P("dp"),
        P("dp"),
        split,
        split,
        split,
        P("groups"),
    )
    return jax.shard_map(
        shards,
        mesh=mesh,
        in_specs=placed,
        out_specs=(split, split),
        check_vma=False,
    )
```

profile of v0, /device:TPU:22, one launch (start us, length us, event | category | flops | bytes accessed | tf_op | source)
XLA Modules:
  0.0 34.2 jit_solution(7587718178806611258)
XLA Ops:
  0.6 0.0 copy-start.1
  0.6 0.0 copy-start.2
  0.7 0.0 copy-start.5
  0.7 0.0 copy-start.8
  0.7 0.0 copy-start.9
  0.7 0.0 copy-start.10
  0.8 2.9 %first_state.1.refs_13_.refs_1_ = bf16[144,1024]{1,0:T(8,128)(2,1)} custom-call(bf16[128,2048]{1,0:T(8,128)(2,1)} %refs_0_.4, bf16[128,512]{1,0:T(8,128)(2,1)} %refs_1_.3, f32[32,128]{1,0:T(8,128)} %bitcast.5, f32[4,2048]{1,0:T(4,128)} %refs_7_.3, f32[1,2048]{1,0:T(1,128)} %bitcast.7, f32[4,512]{1,0:T(4,128)} %refs_8_.3, f32[1,512]{1,0:T(1,128)} %bitcast.8, ...), custom_call_target="tpu_custom_call" | custom-call | flops 2000000000 | bytes 1018128 | tf_op jit(solution)/shard_map/first_state/pallas_call | solution.py:582
  3.7 0.0 copy-start.4
  3.7 0.0 copy-start.6
  3.7 0.0 copy-start.7
  3.7 3.6 %collective-permute-start = (bf16[144,1024]{1,0:T(8,128)(2,1)}, bf16[144,1024]{1,0:T(8,128)(2,1)S(1)}, u32[]{:S(2)}, u32[]{:S(2)}) collective-permute-start(bf16[144,1024]{1,0:T(8,128)(2,1)} %first_state.1.refs_13_.refs_1_), channel_id=1, source_target_pairs={{0,4},{4,8},{8,12},{1,5},{5,9},{9,13},{2,6},{6,10},{10,14},{3,7},{... | collective-permute-start | bytes 884744 | tf_op jit(solution)/shard_map/ppermute | solution.py:598
  7.4 3.6 %prepare.1 = (bf16[128,2048]{1,0:T(8,128)(2,1)}, bf16[128,512]{1,0:T(8,128)(2,1)S(1)}, f32[8,2560]{1,0:T(8,128)S(1)}, f32[8,2048]{1,0:T(8,128)S(1)}, f32[8,2048]...) custom-call(bf16[128,2048]{1,0:T(8,128)(2,1)S(1)} %copy-done.1, ...), custom_call_target="tpu_custom_call" | custom-call | flops 2000000000 | bytes 5728656 | tf_op jit(solution)/shard_map/prepare/pallas_call | solution.py:582
  11.0 0.0 copy-start.3
  11.0 0.8 %attend_own.1 = (f32[128,1024]{1,0:T(8,128)S(1)}, f32[128,1024]{1,0:T(8,128)S(1)}, f32[128,1024]{1,0:T(8,128)S(1)}, bf16[128,512]{1,0:T(8,128)(2,1)S(1)}) custom-call(bf16[128,1024]{1,0:T(8,128)(2,1)S(1)} %copy-done.4, bf16[128,256]{1,0:T(8,128)(2,1)S(1)} %copy-done.6, bf16[128,256]{1,0:T(8,128)(2,1)S(1)} %copy-done.7, ...), custom_call_target="tpu_custom_call" | custom-call | flops 2000000000 | bytes 2162688 | tf_op jit(solution)/shard_map/attend_own/pallas_call | solution.py:582
  11.8 1.9 %collective-permute-start.3 = (bf16[128,512]{1,0:T(8,128)(2,1)S(1)}, bf16[128,512]{1,0:T(8,128)(2,1)S(1)}, u32[]{:S(2)}, u32[]{:S(2)}) collective-permute-start(bf16[128,512]{1,0:T(8,128)(2,1)S(1)} %get-tuple-element.47), channel_id=1, source_target_pairs={{0,4},{4,8},{8,12},{1,5},{5,9},{9,13},{2,6},{6,10},{10,14},{3,7},{... | collective-permute-start | bytes 393224 | tf_op jit(solution)/shard_map/ppermute | solution.py:598
  13.7 0.9 %collective-permute-done.refs_0_.refs_5_ = bf16[144,1024]{1,0:T(8,128)(2,1)S(1)} collective-permute-done((bf16[144,1024]{1,0:T(8,128)(2,1)}, bf16[144,1024]{1,0:T(8,128)(2,1)S(1)}, u32[]{:S(2)}, u32[]{:S(2)}) %collective-permute-start) | collective-permute-done | bytes 294944 | tf_op jit(solution)/shard_map/ppermute | solution.py:598
  14.7 0.3 relay_slot2.1
  15.0 3.5 %collective-permute-start.1 = (bf16[128,1024]{1,0:T(8,128)(2,1)S(1)}, bf16[128,1024]{1,0:T(8,128)(2,1)S(1)}, u32[]{:S(2)}, u32[]{:S(2)}) collective-permute-start(bf16[128,1024]{1,0:T(8,128)(2,1)S(1)} %relay_slot2.1), channel_id=1, source_target_pairs={{0,4},{4,8},{8,12},{1,5},{5,9},{9,13},{2,6},{6,10},{10,14},{3,7},{... | collective-permute-start | bytes 786440 | tf_op jit(solution)/shard_map/ppermute | solution.py:598
  18.6 0.0 copy-start
  18.6 1.2 %first_rows.1 = (f32[128,2048]{1,0:T(8,128)S(1)}, bf16[128,256]{1,0:T(8,128)(2,1)S(1)}, bf16[128,1024]{1,0:T(8,128)(2,1)}, bf16[128,1024]{1,0:T(8,128)(2,1)S(1)}) custom-call(bf16[144,1024]{1,0:T(8,128)(2,1)S(1)} %collective-permute-done.refs_0_.refs_5_, f32[8,2560]{1,0:T(8,128)S(1)} %get-tuple-element.29.refs_1_.refs_2_, ...), custom_call_target="tpu_custom_call" | custom-call | flops 2000000000 | bytes 5095424 | tf_op jit(solution)/shard_map/first_rows/pallas_call | solution.py:582
  19.8 0.0 collective-permute-done.3.before_ref
  19.8 0.8 %attend_near.1 = (f32[128,1024]{1,0:T(8,128)S(1)}, f32[128,1024]{1,0:T(8,128)S(1)}, f32[128,1024]{1,0:T(8,128)S(1)}, bf16[128,512]{1,0:T(8,128)(2,1)S(1)}) custom-call(bf16[128,1024]{1,0:T(8,128)(2,1)S(1)} %copy-done.4, bf16[128,512]{1,0:T(8,128)(2,1)S(1)} %collective-permute-done.3.before_ref, s32[128,128]{1,0:T(8,128)S(1)} %get-tuple-element.35.refs_9_.begin_ref.refs_1_, ...), custom_call_target="tpu_custom_call" | custom-call | flops 2000000000 | bytes 3739648 | tf_op jit(solution)/shard_map/attend_near/pallas_call | solution.py:582
  20.6 1.9 %collective-permute-start.4 = (bf16[128,512]{1,0:T(8,128)(2,1)S(1)}, bf16[128,512]{1,0:T(8,128)(2,1)S(1)}, u32[]{:S(2)}, u32[]{:S(2)}) collective-permute-start(bf16[128,512]{1,0:T(8,128)(2,1)S(1)} %get-tuple-element.55), channel_id=1, source_target_pairs={{4,8},{8,12},{5,9},{9,13},{6,10},{10,14},{7,11},{11,15},{20,24},{2... | collective-permute-start | bytes 393224 | tf_op jit(solution)/shard_map/ppermute | solution.py:598
  22.5 1.8 %collective-permute-done.1.refs_0_.refs_6_.refs_5_ = bf16[128,1024]{1,0:T(8,128)(2,1)S(1)} collective-permute-done((bf16[128,1024]{1,0:T(8,128)(2,1)S(1)}, bf16[128,1024]{1,0:T(8,128)(2,1)S(1)}, u32[]{:S(2)}, u32[]{:S(2)}) %collective-permute-start.1) | collective-permute-done | bytes 262176 | tf_op jit(solution)/shard_map/ppermute | solution.py:598
  24.3 0.1 relay_slot3.1
  24.4 3.9 %collective-permute-start.2 = (bf16[128,1024]{1,0:T(8,128)(2,1)S(1)}, bf16[128,1024]{1,0:T(8,128)(2,1)S(1)}, u32[]{:S(2)}, u32[]{:S(2)}) collective-permute-start(bf16[128,1024]{1,0:T(8,128)(2,1)S(1)} %relay_slot3.1), channel_id=1, source_target_pairs={{4,8},{8,12},{5,9},{9,13},{6,10},{10,14},{7,11},{11,15},{20,24},{2... | collective-permute-start | bytes 786440 | tf_op jit(solution)/shard_map/ppermute | solution.py:598
  28.3 0.0 collective-permute-done.4.refs_5_
  28.3 1.5 %attend_far.1 = bf16[128,1024]{1,0:T(8,128)(2,1)} custom-call(bf16[128,1024]{1,0:T(8,128)(2,1)S(1)} %copy-done.4, s32[128,128]{1,0:T(8,128)S(1)} %get-tuple-element.35.refs_9_.begin_ref.refs_1_, f32[128,1024]{1,0:T(8,128)S(1)} %get-tuple-element.52.refs_2_, f32[128,1024]{1,0:T(8,128)S(1)} %get-tuple-element.53.refs_3_, ...), custom_call_target="tpu_custom_call" | custom-call | flops 2000000000 | bytes 2293760 | tf_op jit(solution)/shard_map/attend_far/pallas_call | solution.py:582
  29.7 1.1 %norm_part0_rest.1.refs_6_ = bf16[128,2048]{1,0:T(8,128)(2,1)} custom-call(f32[128,2048]{1,0:T(8,128)S(1)} %get-tuple-element.40.refs_0_, f32[128,2048]{1,0:T(8,128)S(1)} %get-tuple-element.41.refs_1_, bf16[128,256]{1,0:T(8,128)(2,1)S(1)} %get-tuple-element.42.refs_2_, f32[2048]{0:T(1024)S(1)} %copy-done, ...), custom_call_target="tpu_custom_call", output_to_operand_aliasing={{}: (7, {})} | custom-call | flops 1000000000 | bytes 3792896 | tf_op jit(solution)/shard_map/norm_part0_rest/pallas_call | solution.py:582
  30.8 0.1 norm_part1_first.1.refs_6_
  30.9 2.2 %collective-permute-done.2.refs_5_ = bf16[128,1024]{1,0:T(8,128)(2,1)S(1)} collective-permute-done((bf16[128,1024]{1,0:T(8,128)(2,1)S(1)}, bf16[128,1024]{1,0:T(8,128)(2,1)S(1)}, u32[]{:S(2)}, u32[]{:S(2)}) %collective-permute-start.2) | collective-permute-done | bytes 262176 | tf_op jit(solution)/shard_map/ppermute | solution.py:598
  33.1 1.1 %norm_part1_later.1 = bf16[128,2048]{1,0:T(8,128)(2,1)} custom-call(f32[128,2048]{1,0:T(8,128)S(1)} %get-tuple-element.40.refs_0_, f32[128,2048]{1,0:T(8,128)S(1)} %get-tuple-element.41.refs_1_, bf16[128,256]{1,0:T(8,128)(2,1)S(1)} %get-tuple-element.42.refs_2_, f32[2048]{0:T(1024)S(1)} %copy-done, ...), custom_call_target="tpu_custom_call", output_to_operand_aliasing={{}: (6, {})} | custom-call | flops 1000000000 | bytes 3497984 | tf_op jit(solution)/shard_map/norm_part1_later/pallas_call | solution.py:582
  (24 shorter events, 0.1 us)
Async XLA Ops:
  0.6 6.7 %copy-start.1 = (bf16[128,2048]{1,0:T(8,128)(2,1)S(1)}, bf16[128,2048]{1,0:T(8,128)(2,1)}, u32[]{:S(2)}) copy-start(bf16[128,2048]{1,0:T(8,128)(2,1)} %refs_0_.4) | copy-start | bytes 1572868
  0.6 6.7 %copy-start.2 = (bf16[128,2048]{1,0:T(8,128)(2,1)S(1)}, bf16[128,2048]{1,0:T(8,128)(2,1)}, u32[]{:S(2)}) copy-start(bf16[128,2048]{1,0:T(8,128)(2,1)} %refs_11_.1) | copy-start | bytes 1572868
  0.7 6.7 %copy-start.5 = (bf16[128,512]{1,0:T(8,128)(2,1)S(1)}, bf16[128,512]{1,0:T(8,128)(2,1)}, u32[]{:S(2)}) copy-start(bf16[128,512]{1,0:T(8,128)(2,1)} %refs_1_.3) | copy-start | bytes 393220
  0.7 6.7 %copy-start.8 = (f32[4,2048]{1,0:T(4,128)S(1)}, f32[4,2048]{1,0:T(4,128)}, u32[]{:S(2)}) copy-start(f32[4,2048]{1,0:T(4,128)} %refs_7_.3) | copy-start | bytes 98308
  0.7 6.7 %copy-start.9 = (f32[128,32]{0,1:T(8,128)S(1)}, f32[128,32]{0,1:T(8,128)}, u32[]{:S(2)}) copy-start(f32[128,32]{0,1:T(8,128)} %param.19) | copy-start | bytes 49156
  0.7 6.7 %copy-start.10 = (f32[2048]{0:T(1024)S(1)}, f32[2048]{0:T(1024)}, u32[]{:S(2)}) copy-start(f32[2048]{0:T(1024)} %refs_4_.2) | copy-start | bytes 24580
  0.7 6.7 %copy-start.11 = (f32[4,512]{1,0:T(4,128)S(1)}, f32[4,512]{1,0:T(4,128)}, u32[]{:S(2)}) copy-start(f32[4,512]{1,0:T(4,128)} %refs_8_.3) | copy-start | bytes 24580
  0.7 6.7 %copy-start.12 = (f32[512]{0:T(512)S(1)}, f32[512]{0:T(512)}, u32[]{:S(2)}) copy-start(f32[512]{0:T(512)} %refs_6_.1) | copy-start | bytes 6148
  0.7 6.7 %copy-start.13 = (f32[32]{0:T(128)S(1)}, f32[32]{0:T(128)}, u32[]{:S(2)}) copy-start(f32[32]{0:T(128)} %refs_7_.2) | copy-start | bytes 388
  0.7 6.7 %copy-start.14 = (f32[32]{0:T(128)S(1)}, f32[32]{0:T(128)}, u32[]{:S(2)}) copy-start(f32[32]{0:T(128)} %refs_8_.2) | copy-start | bytes 388
  0.7 6.7 %copy-start.15 = (s32[4]{0:T(128)S(1)}, s32[4]{0:T(128)}, u32[]{:S(2)}) copy-start(s32[4]{0:T(128)} %refs_10_.1) | copy-start | bytes 52
  0.7 6.7 %copy-start.16 = (f32[32]{0:T(128)S(1)}, f32[32]{0:T(128)}, u32[]{:S(2)}) copy-start(f32[32]{0:T(128)} %refs_9_.3) | copy-start | bytes 388
  3.7 7.4 %copy-start.4 = (bf16[128,1024]{1,0:T(8,128)(2,1)S(1)}, bf16[128,1024]{1,0:T(8,128)(2,1)}, u32[]{:S(2)}) copy-start(bf16[128,1024]{1,0:T(8,128)(2,1)} %refs_0_.5) | copy-start | bytes 786436
  3.7 7.3 %copy-start.6 = (bf16[128,256]{1,0:T(8,128)(2,1)S(1)}, bf16[128,256]{1,0:T(8,128)(2,1)}, u32[]{:S(2)}) copy-start(bf16[128,256]{1,0:T(8,128)(2,1)} %keys_ref.1) | copy-start | bytes 196612
  3.7 7.3 %copy-start.7 = (bf16[128,256]{1,0:T(8,128)(2,1)S(1)}, bf16[128,256]{1,0:T(8,128)(2,1)}, u32[]{:S(2)}) copy-start(bf16[128,256]{1,0:T(8,128)(2,1)} %values_ref.1) | copy-start | bytes 196612
  3.7 11.0 %collective-permute-start = (bf16[144,1024]{1,0:T(8,128)(2,1)}, bf16[144,1024]{1,0:T(8,128)(2,1)S(1)}, u32[]{:S(2)}, u32[]{:S(2)}) collective-permute-start(bf16[144,1024]{1,0:T(8,128)(2,1)} %first_state.1.refs_13_.refs_1_), channel_id=1, source_target_pairs={{0,4},{4,8},{8,12},{1,5},{5,9},{9,13},{2,6},{6,10},{10,14},{3,7},{... | collective-permute-start | bytes 884744 | tf_op jit(solution)/shard_map/ppermute | solution.py:598
  11.0 3.7 %copy-start.3 = (bf16[144,1024]{1,0:T(8,128)(2,1)S(1)}, bf16[144,1024]{1,0:T(8,128)(2,1)}, u32[]{:S(2)}) copy-start(bf16[144,1024]{1,0:T(8,128)(2,1)} %first_state.1.refs_13_.refs_1_) | copy-start | bytes 884740
  11.8 8.0 %collective-permute-start.3 = (bf16[128,512]{1,0:T(8,128)(2,1)S(1)}, bf16[128,512]{1,0:T(8,128)(2,1)S(1)}, u32[]{:S(2)}, u32[]{:S(2)}) collective-permute-start(bf16[128,512]{1,0:T(8,128)(2,1)S(1)} %get-tuple-element.47), channel_id=1, source_target_pairs={{0,4},{4,8},{8,12},{1,5},{5,9},{9,13},{2,6},{6,10},{10,14},{3,7},{... | collective-permute-start | bytes 393224 | tf_op jit(solution)/shard_map/ppermute | solution.py:598
  15.0 9.3 %collective-permute-start.1 = (bf16[128,1024]{1,0:T(8,128)(2,1)S(1)}, bf16[128,1024]{1,0:T(8,128)(2,1)S(1)}, u32[]{:S(2)}, u32[]{:S(2)}) collective-permute-start(bf16[128,1024]{1,0:T(8,128)(2,1)S(1)} %relay_slot2.1), channel_id=1, source_target_pairs={{0,4},{4,8},{8,12},{1,5},{5,9},{9,13},{2,6},{6,10},{10,14},{3,7},{... | collective-permute-start | bytes 786440 | tf_op jit(solution)/shard_map/ppermute | solution.py:598
  18.6 1.2 %copy-start = (f32[2048]{0:T(1024)S(1)}, f32[2048]{0:T(1024)}, u32[]{:S(2)}) copy-start(f32[2048]{0:T(1024)} %refs_3_.11) | copy-start | bytes 24580
  20.6 7.7 %collective-permute-start.4 = (bf16[128,512]{1,0:T(8,128)(2,1)S(1)}, bf16[128,512]{1,0:T(8,128)(2,1)S(1)}, u32[]{:S(2)}, u32[]{:S(2)}) collective-permute-start(bf16[128,512]{1,0:T(8,128)(2,1)S(1)} %get-tuple-element.55), channel_id=1, source_target_pairs={{4,8},{8,12},{5,9},{9,13},{6,10},{10,14},{7,11},{11,15},{20,24},{2... | collective-permute-start | bytes 393224 | tf_op jit(solution)/shard_map/ppermute | solution.py:598
  24.4 8.8 %collective-permute-start.2 = (bf16[128,1024]{1,0:T(8,128)(2,1)S(1)}, bf16[128,1024]{1,0:T(8,128)(2,1)S(1)}, u32[]{:S(2)}, u32[]{:S(2)}) collective-permute-start(bf16[128,1024]{1,0:T(8,128)(2,1)S(1)} %relay_slot3.1), channel_id=1, source_target_pairs={{4,8},{8,12},{5,9},{9,13},{6,10},{10,14},{7,11},{11,15},{20,24},{2... | collective-permute-start | bytes 786440 | tf_op jit(solution)/shard_map/ppermute | solution.py:598
where the time goes:
time: 34.4 us; the launch traced here: 34.2 us
  starting transfers between devices  14.9 us (43%)
  Pallas kernels  13.3 us (39%)
  waiting for transfers between devices  4.94 us (14%)
  between operations  0.99 us (3%)
    ppermute x5, starting transfers between devices, onward(): lax.ppermute(value, 'seq', [(source, source + 1) for source in range(firs...  14.9 us
    pallas_call x12, Pallas kernels, call(): pl.pallas_call(kernel, name=name, grid=(1,), out_shape=outs, in_specs=spe...  13.3 us
    ppermute x5, waiting for transfers between devices, onward(): lax.ppermute(value, 'seq', [(source, source + 1) for source in range(firs...  4.94 us
  transfers between devices with their start and end apart: 5, of which 3 were waited for; matrix products, arithmetic and copies ran while one was open for 0% of the time, Pallas kernels for 27%

commit v1 on v0

--- a/solution.py
+++ b/solution.py
@@ -123,7 +123,7 @@
     def corner(ref, shape):
         return ref.at[tuple(pl.ds(0, extent) for extent in shape)]
 
-    order = (0, 9, 2, 7, 8, 1, 5, 6, 3, 4)
+    order = (9, 2, 7, 8, 1, 5, 6, 0, 3, 4)
     copies = {}
     for at in order:
         source = corner(hbm_refs[at], vmem_refs[at].shape)
@@ -323,20 +323,27 @@
     out_ref, pad_ref = refs[-2:]
     width = out_ref.shape[1]
     slots = pad_ref.shape[0]
-    lines = tail_lines(message_ref, STATE)
-    top = functools.partial(first_rows, lines, partial_ref, inside_ref)
-    inputs = top(wbc_ref, pad_ref, 0, wx_ref.shape[1], 0)[:, :STATE]
-    turned = jnp.concatenate([inputs, inputs], axis=0).T.astype(BF16)
-    own = flag_ref[0, 0:1] > 0.5
-    for start in range(0, width, CHUNK):
-        columns = slice(start, start + CHUNK)
-        xc = top(wx_ref, pad_ref, (start // CHUNK + 1) % slots, 0, start)
-        weighted = sixteen(xc * weight_ref[:, columns])
-        full = state_ref[:STATE, columns].astype(F32) + jnp.dot(
-            turned, weighted, preferred_element_type=F32
-        )
-        full = full + through_ref[0:1, columns] * message_ref[:STATE, columns].astype(F32)
-        out_ref[:, columns] = jnp.where(own, other_ref[:STATE, columns].astype(F32), full).astype(BF16)
+    own = flag_ref[0, 0, 0] > 0.5
+
+    @pl.when(own)
+    def _():
+        out_ref[...] = other_ref[:STATE]
+
+    @pl.when(jnp.logical_not(own))
+    def _():
+        lines = tail_lines(message_ref, STATE)
+        top = functools.partial(first_rows, lines, partial_ref, inside_ref)
+        inputs = top(wbc_ref, pad_ref, 0, wx_ref.shape[1], 0)[:, :STATE]
+        turned = jnp.concatenate([inputs, inputs], axis=0).T.astype(BF16)
+        for start in range(0, width, CHUNK):
+            columns = slice(start, start + CHUNK)
+            xc = top(wx_ref, pad_ref, (start // CHUNK + 1) % slots, 0, start)
+            weighted = sixteen(xc * weight_ref[:, columns])
+            full = state_ref[:STATE, columns].astype(F32) + jnp.dot(
+                turned, weighted, preferred_element_type=F32
+            )
+            full = full + through_ref[0:1, columns] * message_ref[:STATE, columns].astype(F32)
+            out_ref[:, columns] = full.astype(BF16)
 
 
 def relay_kernel(part, fresh, *refs):

time: 34.4 us -> 34.3 us (level)
  waiting for transfers between devices: 4.94 us -> 5.32 us
    ppermute x5, waiting for transfers between devices: 4.94 us -> 5.32 us  [onward(): lax.ppermute(value, 'seq', [(source, source + 1) for source in range(firs...]
where the time goes in v1:
time: 34.3 us; the launch traced here: 34 us
  starting transfers between devices  14.6 us (43%)
  Pallas kernels  13 us (38%)
  waiting for transfers between devices  5.32 us (16%)
  between operations  0.99 us (3%)
    ppermute x5, starting transfers between devices, onward(): lax.ppermute(value, 'seq', [(source, source + 1) for source in range(firs...  14.6 us
    pallas_call x12, Pallas kernels, call(): pl.pallas_call(kernel, name=name, grid=(1,), out_shape=outs, in_specs=spe...  13 us
    ppermute x5, waiting for transfers between devices, onward(): lax.ppermute(value, 'seq', [(source, source + 1) for source in range(firs...  5.32 us
  transfers between devices with their start and end apart: 5, of which 3 were waited for; matrix products, arithmetic and copies ran while one was open for 0% of the time, Pallas kernels for 27%

profile of v1, /device:TPU:22, one launch (start us, length us, event | category | flops | bytes accessed | tf_op | source)
XLA Modules:
  0.0 34.0 jit_solution(14064027694265662009)
XLA Ops:
  0.6 0.0 copy-start.1
  0.6 0.0 copy-start.2
  0.7 0.0 copy-start.5
  0.7 0.0 copy-start.8
  0.7 0.0 copy-start.9
  0.7 0.0 copy-start.10
  0.7 0.0 copy-start.11
  0.8 2.8 %first_state.1.refs_13_.refs_1_ = bf16[144,1024]{1,0:T(8,128)(2,1)} custom-call(bf16[128,2048]{1,0:T(8,128)(2,1)} %refs_0_.4, bf16[128,512]{1,0:T(8,128)(2,1)} %refs_1_.3, f32[32,128]{1,0:T(8,128)} %bitcast.5, f32[4,2048]{1,0:T(4,128)} %refs_7_.3, f32[1,2048]{1,0:T(1,128)} %bitcast.7, f32[4,512]{1,0:T(4,128)} %refs_8_.3, f32[1,512]{1,0:T(1,128)} %bitcast.8, ...), custom_call_target="tpu_custom_call" | custom-call | flops 2000000000 | bytes 1018128 | tf_op jit(solution)/shard_map/first_state/pallas_call | solution.py:589
  3.6 0.0 copy-start.4
  3.6 0.0 copy-start.6
  3.6 0.0 copy-start.7
  3.6 3.6 %collective-permute-start = (bf16[144,1024]{1,0:T(8,128)(2,1)}, bf16[144,1024]{1,0:T(8,128)(2,1)S(1)}, u32[]{:S(2)}, u32[]{:S(2)}) collective-permute-start(bf16[144,1024]{1,0:T(8,128)(2,1)} %first_state.1.refs_13_.refs_1_), channel_id=1, source_target_pairs={{0,4},{4,8},{8,12},{1,5},{5,9},{9,13},{2,6},{6,10},{10,14},{3,7},{... | collective-permute-start | bytes 884744 | tf_op jit(solution)/shard_map/ppermute | solution.py:605
  7.4 3.6 %prepare.1 = (bf16[128,2048]{1,0:T(8,128)(2,1)}, bf16[128,512]{1,0:T(8,128)(2,1)S(1)}, f32[8,2560]{1,0:T(8,128)S(1)}, f32[8,2048]{1,0:T(8,128)S(1)}, f32[8,2048]...) custom-call(bf16[128,2048]{1,0:T(8,128)(2,1)S(1)} %copy-done.1, ...), custom_call_target="tpu_custom_call" | custom-call | flops 2000000000 | bytes 5728656 | tf_op jit(solution)/shard_map/prepare/pallas_call | solution.py:589
  11.0 0.8 %attend_own.1 = (f32[128,1024]{1,0:T(8,128)S(1)}, f32[128,1024]{1,0:T(8,128)S(1)}, f32[128,1024]{1,0:T(8,128)S(1)}, bf16[128,512]{1,0:T(8,128)(2,1)S(1)}) custom-call(bf16[128,1024]{1,0:T(8,128)(2,1)S(1)} %copy-done.4, bf16[128,256]{1,0:T(8,128)(2,1)S(1)} %copy-done.6, bf16[128,256]{1,0:T(8,128)(2,1)S(1)} %copy-done.7, ...), custom_call_target="tpu_custom_call" | custom-call | flops 2000000000 | bytes 2162688 | tf_op jit(solution)/shard_map/attend_own/pallas_call | solution.py:589
  11.7 1.9 %collective-permute-start.3 = (bf16[128,512]{1,0:T(8,128)(2,1)S(1)}, bf16[128,512]{1,0:T(8,128)(2,1)S(1)}, u32[]{:S(2)}, u32[]{:S(2)}) collective-permute-start(bf16[128,512]{1,0:T(8,128)(2,1)S(1)} %get-tuple-element.47), channel_id=1, source_target_pairs={{0,4},{4,8},{8,12},{1,5},{5,9},{9,13},{2,6},{6,10},{10,14},{3,7},{... | collective-permute-start | bytes 393224 | tf_op jit(solution)/shard_map/ppermute | solution.py:605
  13.7 0.9 %collective-permute-done.refs_0_.refs_5_ = bf16[144,1024]{1,0:T(8,128)(2,1)S(1)} collective-permute-done((bf16[144,1024]{1,0:T(8,128)(2,1)}, bf16[144,1024]{1,0:T(8,128)(2,1)S(1)}, u32[]{:S(2)}, u32[]{:S(2)}) %collective-permute-start) | collective-permute-done | bytes 294944 | tf_op jit(solution)/shard_map/ppermute | solution.py:605
  14.6 0.1 relay_slot2.1
  14.7 3.5 %collective-permute-start.1 = (bf16[128,1024]{1,0:T(8,128)(2,1)S(1)}, bf16[128,1024]{1,0:T(8,128)(2,1)S(1)}, u32[]{:S(2)}, u32[]{:S(2)}) collective-permute-start(bf16[128,1024]{1,0:T(8,128)(2,1)S(1)} %relay_slot2.1), channel_id=1, source_target_pairs={{0,4},{4,8},{8,12},{1,5},{5,9},{9,13},{2,6},{6,10},{10,14},{3,7},{... | collective-permute-start | bytes 786440 | tf_op jit(solution)/shard_map/ppermute | solution.py:605
  18.2 0.0 copy-start
  18.2 1.2 %first_rows.1 = (f32[128,2048]{1,0:T(8,128)S(1)}, bf16[128,256]{1,0:T(8,128)(2,1)S(1)}, bf16[128,1024]{1,0:T(8,128)(2,1)}, bf16[128,1024]{1,0:T(8,128)(2,1)S(1)}) custom-call(bf16[144,1024]{1,0:T(8,128)(2,1)S(1)} %collective-permute-done.refs_0_.refs_5_, f32[8,2560]{1,0:T(8,128)S(1)} %get-tuple-element.29.refs_1_.refs_2_, ...), custom_call_target="tpu_custom_call" | custom-call | flops 2000000000 | bytes 5095424 | tf_op jit(solution)/shard_map/first_rows/pallas_call | solution.py:589
  19.5 0.0 collective-permute-done.3.before_ref
  19.5 0.8 %attend_near.1 = (f32[128,1024]{1,0:T(8,128)S(1)}, f32[128,1024]{1,0:T(8,128)S(1)}, f32[128,1024]{1,0:T(8,128)S(1)}, bf16[128,512]{1,0:T(8,128)(2,1)S(1)}) custom-call(bf16[128,1024]{1,0:T(8,128)(2,1)S(1)} %copy-done.4, bf16[128,512]{1,0:T(8,128)(2,1)S(1)} %collective-permute-done.3.before_ref, s32[128,128]{1,0:T(8,128)S(1)} %get-tuple-element.35.refs_9_.begin_ref.refs_1_, ...), custom_call_target="tpu_custom_call" | custom-call | flops 2000000000 | bytes 3739648 | tf_op jit(solution)/shard_map/attend_near/pallas_call | solution.py:589
  20.2 1.9 %collective-permute-start.4 = (bf16[128,512]{1,0:T(8,128)(2,1)S(1)}, bf16[128,512]{1,0:T(8,128)(2,1)S(1)}, u32[]{:S(2)}, u32[]{:S(2)}) collective-permute-start(bf16[128,512]{1,0:T(8,128)(2,1)S(1)} %get-tuple-element.55), channel_id=1, source_target_pairs={{4,8},{8,12},{5,9},{9,13},{6,10},{10,14},{7,11},{11,15},{20,24},{2... | collective-permute-start | bytes 393224 | tf_op jit(solution)/shard_map/ppermute | solution.py:605
  22.2 2.1 %collective-permute-done.1.refs_0_.refs_6_.refs_5_ = bf16[128,1024]{1,0:T(8,128)(2,1)S(1)} collective-permute-done((bf16[128,1024]{1,0:T(8,128)(2,1)S(1)}, bf16[128,1024]{1,0:T(8,128)(2,1)S(1)}, u32[]{:S(2)}, u32[]{:S(2)}) %collective-permute-start.1) | collective-permute-done | bytes 262176 | tf_op jit(solution)/shard_map/ppermute | solution.py:605
  24.2 0.1 relay_slot3.1
  24.3 3.6 %collective-permute-start.2 = (bf16[128,1024]{1,0:T(8,128)(2,1)S(1)}, bf16[128,1024]{1,0:T(8,128)(2,1)S(1)}, u32[]{:S(2)}, u32[]{:S(2)}) collective-permute-start(bf16[128,1024]{1,0:T(8,128)(2,1)S(1)} %relay_slot3.1), channel_id=1, source_target_pairs={{4,8},{8,12},{5,9},{9,13},{6,10},{10,14},{7,11},{11,15},{20,24},{2... | collective-permute-start | bytes 786440 | tf_op jit(solution)/shard_map/ppermute | solution.py:605
  27.9 0.0 collective-permute-done.4.refs_5_
  27.9 1.5 %attend_far.1 = bf16[128,1024]{1,0:T(8,128)(2,1)} custom-call(bf16[128,1024]{1,0:T(8,128)(2,1)S(1)} %copy-done.4, s32[128,128]{1,0:T(8,128)S(1)} %get-tuple-element.35.refs_9_.begin_ref.refs_1_, f32[128,1024]{1,0:T(8,128)S(1)} %get-tuple-element.52.refs_2_, f32[128,1024]{1,0:T(8,128)S(1)} %get-tuple-element.53.refs_3_, ...), custom_call_target="tpu_custom_call" | custom-call | flops 2000000000 | bytes 2293760 | tf_op jit(solution)/shard_map/attend_far/pallas_call | solution.py:589
  29.4 1.1 %norm_part0_rest.1.refs_6_ = bf16[128,2048]{1,0:T(8,128)(2,1)} custom-call(f32[128,2048]{1,0:T(8,128)S(1)} %get-tuple-element.40.refs_0_, f32[128,2048]{1,0:T(8,128)S(1)} %get-tuple-element.41.refs_1_, bf16[128,256]{1,0:T(8,128)(2,1)S(1)} %get-tuple-element.42.refs_2_, f32[2048]{0:T(1024)S(1)} %copy-done, ...), custom_call_target="tpu_custom_call", output_to_operand_aliasing={{}: (7, {})} | custom-call | flops 1000000000 | bytes 3792896 | tf_op jit(solution)/shard_map/norm_part0_rest/pallas_call | solution.py:589
  30.5 0.1 norm_part1_first.1.refs_6_
  30.6 2.3 %collective-permute-done.2.refs_5_ = bf16[128,1024]{1,0:T(8,128)(2,1)S(1)} collective-permute-done((bf16[128,1024]{1,0:T(8,128)(2,1)S(1)}, bf16[128,1024]{1,0:T(8,128)(2,1)S(1)}, u32[]{:S(2)}, u32[]{:S(2)}) %collective-permute-start.2) | collective-permute-done | bytes 262176 | tf_op jit(solution)/shard_map/ppermute | solution.py:605
  32.9 1.1 %norm_part1_later.1 = bf16[128,2048]{1,0:T(8,128)(2,1)} custom-call(f32[128,2048]{1,0:T(8,128)S(1)} %get-tuple-element.40.refs_0_, f32[128,2048]{1,0:T(8,128)S(1)} %get-tuple-element.41.refs_1_, bf16[128,256]{1,0:T(8,128)(2,1)S(1)} %get-tuple-element.42.refs_2_, f32[2048]{0:T(1024)S(1)} %copy-done, ...), custom_call_target="tpu_custom_call", output_to_operand_aliasing={{}: (6, {})} | custom-call | flops 1000000000 | bytes 3497984 | tf_op jit(solution)/shard_map/norm_part1_later/pallas_call | solution.py:589
  (24 shorter events, 0.1 us)
Async XLA Ops:
  0.6 6.6 %copy-start.1 = (bf16[128,2048]{1,0:T(8,128)(2,1)S(1)}, bf16[128,2048]{1,0:T(8,128)(2,1)}, u32[]{:S(2)}) copy-start(bf16[128,2048]{1,0:T(8,128)(2,1)} %refs_0_.4) | copy-start | bytes 1572868
  0.6 6.6 %copy-start.2 = (bf16[128,2048]{1,0:T(8,128)(2,1)S(1)}, bf16[128,2048]{1,0:T(8,128)(2,1)}, u32[]{:S(2)}) copy-start(bf16[128,2048]{1,0:T(8,128)(2,1)} %refs_11_.1) | copy-start | bytes 1572868
  0.7 6.6 %copy-start.5 = (bf16[128,512]{1,0:T(8,128)(2,1)S(1)}, bf16[128,512]{1,0:T(8,128)(2,1)}, u32[]{:S(2)}) copy-start(bf16[128,512]{1,0:T(8,128)(2,1)} %refs_1_.3) | copy-start | bytes 393220
  0.7 6.6 %copy-start.8 = (f32[4,2048]{1,0:T(4,128)S(1)}, f32[4,2048]{1,0:T(4,128)}, u32[]{:S(2)}) copy-start(f32[4,2048]{1,0:T(4,128)} %refs_7_.3) | copy-start | bytes 98308
  0.7 6.6 %copy-start.9 = (f32[128,32]{0,1:T(8,128)S(1)}, f32[128,32]{0,1:T(8,128)}, u32[]{:S(2)}) copy-start(f32[128,32]{0,1:T(8,128)} %param.19) | copy-start | bytes 49156
  0.7 6.6 %copy-start.10 = (f32[2048]{0:T(1024)S(1)}, f32[2048]{0:T(1024)}, u32[]{:S(2)}) copy-start(f32[2048]{0:T(1024)} %refs_4_.2) | copy-start | bytes 24580
  0.7 6.6 %copy-start.11 = (f32[4,512]{1,0:T(4,128)S(1)}, f32[4,512]{1,0:T(4,128)}, u32[]{:S(2)}) copy-start(f32[4,512]{1,0:T(4,128)} %refs_8_.3) | copy-start | bytes 24580
  0.7 6.6 %copy-start.12 = (f32[512]{0:T(512)S(1)}, f32[512]{0:T(512)}, u32[]{:S(2)}) copy-start(f32[512]{0:T(512)} %refs_6_.1) | copy-start | bytes 6148
  0.7 6.6 %copy-start.13 = (f32[32]{0:T(128)S(1)}, f32[32]{0:T(128)}, u32[]{:S(2)}) copy-start(f32[32]{0:T(128)} %refs_7_.2) | copy-start | bytes 388
  0.7 6.6 %copy-start.14 = (f32[32]{0:T(128)S(1)}, f32[32]{0:T(128)}, u32[]{:S(2)}) copy-start(f32[32]{0:T(128)} %refs_8_.2) | copy-start | bytes 388
  0.7 6.6 %copy-start.15 = (s32[4]{0:T(128)S(1)}, s32[4]{0:T(128)}, u32[]{:S(2)}) copy-start(s32[4]{0:T(128)} %refs_10_.1) | copy-start | bytes 52
  0.7 6.6 %copy-start.16 = (f32[32]{0:T(128)S(1)}, f32[32]{0:T(128)}, u32[]{:S(2)}) copy-start(f32[32]{0:T(128)} %refs_9_.3) | copy-start | bytes 388
  3.6 7.4 %copy-start.4 = (bf16[128,1024]{1,0:T(8,128)(2,1)S(1)}, bf16[128,1024]{1,0:T(8,128)(2,1)}, u32[]{:S(2)}) copy-start(bf16[128,1024]{1,0:T(8,128)(2,1)} %refs_0_.5) | copy-start | bytes 786436
  3.6 7.3 %copy-start.6 = (bf16[128,256]{1,0:T(8,128)(2,1)S(1)}, bf16[128,256]{1,0:T(8,128)(2,1)}, u32[]{:S(2)}) copy-start(bf16[128,256]{1,0:T(8,128)(2,1)} %keys_ref.1) | copy-start | bytes 196612
  3.6 7.3 %copy-start.7 = (bf16[128,256]{1,0:T(8,128)(2,1)S(1)}, bf16[128,256]{1,0:T(8,128)(2,1)}, u32[]{:S(2)}) copy-start(bf16[128,256]{1,0:T(8,128)(2,1)} %values_ref.1) | copy-start | bytes 196612
  3.6 11.0 %collective-permute-start = (bf16[144,1024]{1,0:T(8,128)(2,1)}, bf16[144,1024]{1,0:T(8,128)(2,1)S(1)}, u32[]{:S(2)}, u32[]{:S(2)}) collective-permute-start(bf16[144,1024]{1,0:T(8,128)(2,1)} %first_state.1.refs_13_.refs_1_), channel_id=1, source_target_pairs={{0,4},{4,8},{8,12},{1,5},{5,9},{9,13},{2,6},{6,10},{10,14},{3,7},{... | collective-permute-start | bytes 884744 | tf_op jit(solution)/shard_map/ppermute | solution.py:605
  11.0 3.7 %copy-start.3 = (bf16[144,1024]{1,0:T(8,128)(2,1)S(1)}, bf16[144,1024]{1,0:T(8,128)(2,1)}, u32[]{:S(2)}) copy-start(bf16[144,1024]{1,0:T(8,128)(2,1)} %first_state.1.refs_13_.refs_1_) | copy-start | bytes 884740
  11.7 7.7 %collective-permute-start.3 = (bf16[128,512]{1,0:T(8,128)(2,1)S(1)}, bf16[128,512]{1,0:T(8,128)(2,1)S(1)}, u32[]{:S(2)}, u32[]{:S(2)}) collective-permute-start(bf16[128,512]{1,0:T(8,128)(2,1)S(1)} %get-tuple-element.47), channel_id=1, source_target_pairs={{0,4},{4,8},{8,12},{1,5},{5,9},{9,13},{2,6},{6,10},{10,14},{3,7},{... | collective-permute-start | bytes 393224 | tf_op jit(solution)/shard_map/ppermute | solution.py:605
  14.7 9.5 %collective-permute-start.1 = (bf16[128,1024]{1,0:T(8,128)(2,1)S(1)}, bf16[128,1024]{1,0:T(8,128)(2,1)S(1)}, u32[]{:S(2)}, u32[]{:S(2)}) collective-permute-start(bf16[128,1024]{1,0:T(8,128)(2,1)S(1)} %relay_slot2.1), channel_id=1, source_target_pairs={{0,4},{4,8},{8,12},{1,5},{5,9},{9,13},{2,6},{6,10},{10,14},{3,7},{... | collective-permute-start | bytes 786440 | tf_op jit(solution)/shard_map/ppermute | solution.py:605
  18.2 1.2 %copy-start = (f32[2048]{0:T(1024)S(1)}, f32[2048]{0:T(1024)}, u32[]{:S(2)}) copy-start(f32[2048]{0:T(1024)} %refs_3_.11) | copy-start | bytes 24580
  20.2 7.7 %collective-permute-start.4 = (bf16[128,512]{1,0:T(8,128)(2,1)S(1)}, bf16[128,512]{1,0:T(8,128)(2,1)S(1)}, u32[]{:S(2)}, u32[]{:S(2)}) collective-permute-start(bf16[128,512]{1,0:T(8,128)(2,1)S(1)} %get-tuple-element.55), channel_id=1, source_target_pairs={{4,8},{8,12},{5,9},{9,13},{6,10},{10,14},{7,11},{11,15},{20,24},{2... | collective-permute-start | bytes 393224 | tf_op jit(solution)/shard_map/ppermute | solution.py:605
  24.3 8.6 %collective-permute-start.2 = (bf16[128,1024]{1,0:T(8,128)(2,1)S(1)}, bf16[128,1024]{1,0:T(8,128)(2,1)S(1)}, u32[]{:S(2)}, u32[]{:S(2)}) collective-permute-start(bf16[128,1024]{1,0:T(8,128)(2,1)S(1)} %relay_slot3.1), channel_id=1, source_target_pairs={{4,8},{8,12},{5,9},{9,13},{6,10},{10,14},{7,11},{11,15},{20,24},{2... | collective-permute-start | bytes 786440 | tf_op jit(solution)/shard_map/ppermute | solution.py:605

commit v2 on v1

--- a/solution.py
+++ b/solution.py
@@ -180,7 +180,7 @@
         copy.wait()
 
 
-def prepare_kernel(hops, groups, *refs):
+def prepare_kernel(hops, groups, count, *refs):
     x_ref, bc_ref, dt_ref, wx_ref, bx_ref, wbc_ref, bbc_ref, dt_bias_ref, a_log_ref, skip_ref, lens_ref = refs[:11]
     z_ref = refs[11]
     xc_ref, bcc_ref, partial_ref, weight_ref, through_ref, inside_ref, flag_ref = refs[12:19]
@@ -219,7 +219,7 @@
     inside = [mask[:8] for mask in inside]
     for lag in range(1, taps):
         inside_ref[lag - 1] = inside[lag].astype(F32)
-    flag_ref[0] = jnp.broadcast_to(own.astype(F32), (8, CHUNK))
+    flag_ref[0] = jnp.broadcast_to((own | (here == count - 1)).astype(F32), (8, CHUNK))
     before = reach(here - 1, rows, lens_ref)
     for hop in range(1, hops):
         flag_ref[hop] = jnp.broadcast_to((before == hop).astype(F32), (8, CHUNK))
@@ -668,7 +668,7 @@
     )
     slots = [onward(message)]
     prepared = call(
-        functools.partial(prepare_kernel, hops, groups),
+        functools.partial(prepare_kernel, hops, groups, count),
         "prepare",
         [
             shape((rows, width), BF16),

time: 34.3 us -> 34.3 us (level)
  no operation moved by 1% of the time
where the time goes in v2:
time: 34.3 us; the launch traced here: 34 us
  starting transfers between devices  14.6 us (43%)
  Pallas kernels  13 us (38%)
  waiting for transfers between devices  5.35 us (16%)
  between operations  0.99 us (3%)
    ppermute x5, starting transfers between devices, onward(): lax.ppermute(value, 'seq', [(source, source + 1) for source in range(firs...  14.6 us
    pallas_call x12, Pallas kernels, call(): pl.pallas_call(kernel, name=name, grid=(1,), out_shape=outs, in_specs=spe...  13 us
    ppermute x5, waiting for transfers between devices, onward(): lax.ppermute(value, 'seq', [(source, source + 1) for source in range(firs...  5.35 us
  transfers between devices with their start and end apart: 5, of which 3 were waited for; matrix products, arithmetic and copies ran while one was open for 0% of the time, Pallas kernels for 27%

profile of v2, /device:TPU:22, one launch (start us, length us, event | category | flops | bytes accessed | tf_op | source)
XLA Modules:
  0.0 34.0 jit_solution(15767138227352956757)
XLA Ops:
  0.6 0.0 copy-start.1
  0.6 0.0 copy-start.2
  0.7 0.0 copy-start.5
  0.7 0.0 copy-start.8
  0.7 0.0 copy-start.9
  0.8 2.8 %first_state.1.refs_13_.refs_1_ = bf16[144,1024]{1,0:T(8,128)(2,1)} custom-call(bf16[128,2048]{1,0:T(8,128)(2,1)} %refs_0_.4, bf16[128,512]{1,0:T(8,128)(2,1)} %refs_1_.3, f32[32,128]{1,0:T(8,128)} %bitcast.5, f32[4,2048]{1,0:T(4,128)} %refs_7_.3, f32[1,2048]{1,0:T(1,128)} %bitcast.7, f32[4,512]{1,0:T(4,128)} %refs_8_.3, f32[1,512]{1,0:T(1,128)} %bitcast.8, ...), custom_call_target="tpu_custom_call" | custom-call | flops 2000000000 | bytes 1018128 | tf_op jit(solution)/shard_map/first_state/pallas_call | solution.py:589
  3.6 0.0 copy-start.4
  3.6 0.0 copy-start.6
  3.6 0.0 copy-start.7
  3.6 3.6 %collective-permute-start = (bf16[144,1024]{1,0:T(8,128)(2,1)}, bf16[144,1024]{1,0:T(8,128)(2,1)S(1)}, u32[]{:S(2)}, u32[]{:S(2)}) collective-permute-start(bf16[144,1024]{1,0:T(8,128)(2,1)} %first_state.1.refs_13_.refs_1_), channel_id=1, source_target_pairs={{0,4},{4,8},{8,12},{1,5},{5,9},{9,13},{2,6},{6,10},{10,14},{3,7},{... | collective-permute-start | bytes 884744 | tf_op jit(solution)/shard_map/ppermute | solution.py:605
  7.4 3.6 %prepare.1 = (bf16[128,2048]{1,0:T(8,128)(2,1)}, bf16[128,512]{1,0:T(8,128)(2,1)S(1)}, f32[8,2560]{1,0:T(8,128)S(1)}, f32[8,2048]{1,0:T(8,128)S(1)}, f32[8,2048]...) custom-call(bf16[128,2048]{1,0:T(8,128)(2,1)S(1)} %copy-done.1, ...), custom_call_target="tpu_custom_call" | custom-call | flops 2000000000 | bytes 5728656 | tf_op jit(solution)/shard_map/prepare/pallas_call | solution.py:589
  11.0 0.0 copy-done.4
  11.0 0.8 %attend_own.1 = (f32[128,1024]{1,0:T(8,128)S(1)}, f32[128,1024]{1,0:T(8,128)S(1)}, f32[128,1024]{1,0:T(8,128)S(1)}, bf16[128,512]{1,0:T(8,128)(2,1)S(1)}) custom-call(bf16[128,1024]{1,0:T(8,128)(2,1)S(1)} %copy-done.4, bf16[128,256]{1,0:T(8,128)(2,1)S(1)} %copy-done.6, bf16[128,256]{1,0:T(8,128)(2,1)S(1)} %copy-done.7, ...), custom_call_target="tpu_custom_call" | custom-call | flops 2000000000 | bytes 2162688 | tf_op jit(solution)/shard_map/attend_own/pallas_call | solution.py:589
  11.8 1.9 %collective-permute-start.3 = (bf16[128,512]{1,0:T(8,128)(2,1)S(1)}, bf16[128,512]{1,0:T(8,128)(2,1)S(1)}, u32[]{:S(2)}, u32[]{:S(2)}) collective-permute-start(bf16[128,512]{1,0:T(8,128)(2,1)S(1)} %get-tuple-element.47), channel_id=1, source_target_pairs={{0,4},{4,8},{8,12},{1,5},{5,9},{9,13},{2,6},{6,10},{10,14},{3,7},{... | collective-permute-start | bytes 393224 | tf_op jit(solution)/shard_map/ppermute | solution.py:605
  13.7 0.9 %collective-permute-done.refs_0_.refs_5_ = bf16[144,1024]{1,0:T(8,128)(2,1)S(1)} collective-permute-done((bf16[144,1024]{1,0:T(8,128)(2,1)}, bf16[144,1024]{1,0:T(8,128)(2,1)S(1)}, u32[]{:S(2)}, u32[]{:S(2)}) %collective-permute-start) | collective-permute-done | bytes 294944 | tf_op jit(solution)/shard_map/ppermute | solution.py:605
  14.6 0.1 relay_slot2.1
  14.7 3.5 %collective-permute-start.1 = (bf16[128,1024]{1,0:T(8,128)(2,1)S(1)}, bf16[128,1024]{1,0:T(8,128)(2,1)S(1)}, u32[]{:S(2)}, u32[]{:S(2)}) collective-permute-start(bf16[128,1024]{1,0:T(8,128)(2,1)S(1)} %relay_slot2.1), channel_id=1, source_target_pairs={{0,4},{4,8},{8,12},{1,5},{5,9},{9,13},{2,6},{6,10},{10,14},{3,7},{... | collective-permute-start | bytes 786440 | tf_op jit(solution)/shard_map/ppermute | solution.py:605
  18.2 0.0 copy-start
  18.2 1.2 %first_rows.1 = (f32[128,2048]{1,0:T(8,128)S(1)}, bf16[128,256]{1,0:T(8,128)(2,1)S(1)}, bf16[128,1024]{1,0:T(8,128)(2,1)}, bf16[128,1024]{1,0:T(8,128)(2,1)S(1)}) custom-call(bf16[144,1024]{1,0:T(8,128)(2,1)S(1)} %collective-permute-done.refs_0_.refs_5_, f32[8,2560]{1,0:T(8,128)S(1)} %get-tuple-element.29.refs_1_.refs_2_, ...), custom_call_target="tpu_custom_call" | custom-call | flops 2000000000 | bytes 5095424 | tf_op jit(solution)/shard_map/first_rows/pallas_call | solution.py:589
  19.4 0.0 copy-done
  19.4 0.0 collective-permute-done.3.before_ref
  19.5 0.8 %attend_near.1 = (f32[128,1024]{1,0:T(8,128)S(1)}, f32[128,1024]{1,0:T(8,128)S(1)}, f32[128,1024]{1,0:T(8,128)S(1)}, bf16[128,512]{1,0:T(8,128)(2,1)S(1)}) custom-call(bf16[128,1024]{1,0:T(8,128)(2,1)S(1)} %copy-done.4, bf16[128,512]{1,0:T(8,128)(2,1)S(1)} %collective-permute-done.3.before_ref, s32[128,128]{1,0:T(8,128)S(1)} %get-tuple-element.35.refs_9_.begin_ref.refs_1_, ...), custom_call_target="tpu_custom_call" | custom-call | flops 2000000000 | bytes 3739648 | tf_op jit(solution)/shard_map/attend_near/pallas_call | solution.py:589
  20.2 1.9 %collective-permute-start.4 = (bf16[128,512]{1,0:T(8,128)(2,1)S(1)}, bf16[128,512]{1,0:T(8,128)(2,1)S(1)}, u32[]{:S(2)}, u32[]{:S(2)}) collective-permute-start(bf16[128,512]{1,0:T(8,128)(2,1)S(1)} %get-tuple-element.55), channel_id=1, source_target_pairs={{4,8},{8,12},{5,9},{9,13},{6,10},{10,14},{7,11},{11,15},{20,24},{2... | collective-permute-start | bytes 393224 | tf_op jit(solution)/shard_map/ppermute | solution.py:605
  22.2 2.1 %collective-permute-done.1.refs_0_.refs_6_.refs_5_ = bf16[128,1024]{1,0:T(8,128)(2,1)S(1)} collective-permute-done((bf16[128,1024]{1,0:T(8,128)(2,1)S(1)}, bf16[128,1024]{1,0:T(8,128)(2,1)S(1)}, u32[]{:S(2)}, u32[]{:S(2)}) %collective-permute-start.1) | collective-permute-done | bytes 262176 | tf_op jit(solution)/shard_map/ppermute | solution.py:605
  24.2 0.1 relay_slot3.1
  24.3 3.6 %collective-permute-start.2 = (bf16[128,1024]{1,0:T(8,128)(2,1)S(1)}, bf16[128,1024]{1,0:T(8,128)(2,1)S(1)}, u32[]{:S(2)}, u32[]{:S(2)}) collective-permute-start(bf16[128,1024]{1,0:T(8,128)(2,1)S(1)} %relay_slot3.1), channel_id=1, source_target_pairs={{4,8},{8,12},{5,9},{9,13},{6,10},{10,14},{7,11},{11,15},{20,24},{2... | collective-permute-start | bytes 786440 | tf_op jit(solution)/shard_map/ppermute | solution.py:605
  27.9 0.0 collective-permute-done.4.refs_5_
  27.9 1.5 %attend_far.1 = bf16[128,1024]{1,0:T(8,128)(2,1)} custom-call(bf16[128,1024]{1,0:T(8,128)(2,1)S(1)} %copy-done.4, s32[128,128]{1,0:T(8,128)S(1)} %get-tuple-element.35.refs_9_.begin_ref.refs_1_, f32[128,1024]{1,0:T(8,128)S(1)} %get-tuple-element.52.refs_2_, f32[128,1024]{1,0:T(8,128)S(1)} %get-tuple-element.53.refs_3_, ...), custom_call_target="tpu_custom_call" | custom-call | flops 2000000000 | bytes 2293760 | tf_op jit(solution)/shard_map/attend_far/pallas_call | solution.py:589
  29.4 1.1 %norm_part0_rest.1.refs_6_ = bf16[128,2048]{1,0:T(8,128)(2,1)} custom-call(f32[128,2048]{1,0:T(8,128)S(1)} %get-tuple-element.40.refs_0_, f32[128,2048]{1,0:T(8,128)S(1)} %get-tuple-element.41.refs_1_, bf16[128,256]{1,0:T(8,128)(2,1)S(1)} %get-tuple-element.42.refs_2_, f32[2048]{0:T(1024)S(1)} %copy-done, ...), custom_call_target="tpu_custom_call", output_to_operand_aliasing={{}: (7, {})} | custom-call | flops 1000000000 | bytes 3792896 | tf_op jit(solution)/shard_map/norm_part0_rest/pallas_call | solution.py:589
  30.5 0.1 norm_part1_first.1.refs_6_
  30.6 2.3 %collective-permute-done.2.refs_5_ = bf16[128,1024]{1,0:T(8,128)(2,1)S(1)} collective-permute-done((bf16[128,1024]{1,0:T(8,128)(2,1)S(1)}, bf16[128,1024]{1,0:T(8,128)(2,1)S(1)}, u32[]{:S(2)}, u32[]{:S(2)}) %collective-permute-start.2) | collective-permute-done | bytes 262176 | tf_op jit(solution)/shard_map/ppermute | solution.py:605
  32.9 1.1 %norm_part1_later.1 = bf16[128,2048]{1,0:T(8,128)(2,1)} custom-call(f32[128,2048]{1,0:T(8,128)S(1)} %get-tuple-element.40.refs_0_, f32[128,2048]{1,0:T(8,128)S(1)} %get-tuple-element.41.refs_1_, bf16[128,256]{1,0:T(8,128)(2,1)S(1)} %get-tuple-element.42.refs_2_, f32[2048]{0:T(1024)S(1)} %copy-done, ...), custom_call_target="tpu_custom_call", output_to_operand_aliasing={{}: (6, {})} | custom-call | flops 1000000000 | bytes 3497984 | tf_op jit(solution)/shard_map/norm_part1_later/pallas_call | solution.py:589
  (24 shorter events, 0.1 us)
Async XLA Ops:
  0.6 6.6 %copy-start.1 = (bf16[128,2048]{1,0:T(8,128)(2,1)S(1)}, bf16[128,2048]{1,0:T(8,128)(2,1)}, u32[]{:S(2)}) copy-start(bf16[128,2048]{1,0:T(8,128)(2,1)} %refs_0_.4) | copy-start | bytes 1572868
  0.6 6.6 %copy-start.2 = (bf16[128,2048]{1,0:T(8,128)(2,1)S(1)}, bf16[128,2048]{1,0:T(8,128)(2,1)}, u32[]{:S(2)}) copy-start(bf16[128,2048]{1,0:T(8,128)(2,1)} %refs_11_.1) | copy-start | bytes 1572868
  0.7 6.6 %copy-start.5 = (bf16[128,512]{1,0:T(8,128)(2,1)S(1)}, bf16[128,512]{1,0:T(8,128)(2,1)}, u32[]{:S(2)}) copy-start(bf16[128,512]{1,0:T(8,128)(2,1)} %refs_1_.3) | copy-start | bytes 393220
  0.7 6.6 %copy-start.8 = (f32[4,2048]{1,0:T(4,128)S(1)}, f32[4,2048]{1,0:T(4,128)}, u32[]{:S(2)}) copy-start(f32[4,2048]{1,0:T(4,128)} %refs_7_.3) | copy-start | bytes 98308
  0.7 6.6 %copy-start.9 = (f32[128,32]{0,1:T(8,128)S(1)}, f32[128,32]{0,1:T(8,128)}, u32[]{:S(2)}) copy-start(f32[128,32]{0,1:T(8,128)} %param.19) | copy-start | bytes 49156
  0.7 6.6 %copy-start.10 = (f32[2048]{0:T(1024)S(1)}, f32[2048]{0:T(1024)}, u32[]{:S(2)}) copy-start(f32[2048]{0:T(1024)} %refs_4_.2) | copy-start | bytes 24580
  0.7 6.6 %copy-start.11 = (f32[4,512]{1,0:T(4,128)S(1)}, f32[4,512]{1,0:T(4,128)}, u32[]{:S(2)}) copy-start(f32[4,512]{1,0:T(4,128)} %refs_8_.3) | copy-start | bytes 24580
  0.7 6.6 %copy-start.12 = (f32[512]{0:T(512)S(1)}, f32[512]{0:T(512)}, u32[]{:S(2)}) copy-start(f32[512]{0:T(512)} %refs_6_.1) | copy-start | bytes 6148
  0.7 6.6 %copy-start.13 = (f32[32]{0:T(128)S(1)}, f32[32]{0:T(128)}, u32[]{:S(2)}) copy-start(f32[32]{0:T(128)} %refs_7_.2) | copy-start | bytes 388
  0.7 6.6 %copy-start.14 = (f32[32]{0:T(128)S(1)}, f32[32]{0:T(128)}, u32[]{:S(2)}) copy-start(f32[32]{0:T(128)} %refs_8_.2) | copy-start | bytes 388
  0.7 6.6 %copy-start.15 = (s32[4]{0:T(128)S(1)}, s32[4]{0:T(128)}, u32[]{:S(2)}) copy-start(s32[4]{0:T(128)} %refs_10_.1) | copy-start | bytes 52
  0.7 6.6 %copy-start.16 = (f32[32]{0:T(128)S(1)}, f32[32]{0:T(128)}, u32[]{:S(2)}) copy-start(f32[32]{0:T(128)} %refs_9_.3) | copy-start | bytes 388
  3.6 7.4 %copy-start.4 = (bf16[128,1024]{1,0:T(8,128)(2,1)S(1)}, bf16[128,1024]{1,0:T(8,128)(2,1)}, u32[]{:S(2)}) copy-start(bf16[128,1024]{1,0:T(8,128)(2,1)} %refs_0_.5) | copy-start | bytes 786436
  3.6 7.4 %copy-start.6 = (bf16[128,256]{1,0:T(8,128)(2,1)S(1)}, bf16[128,256]{1,0:T(8,128)(2,1)}, u32[]{:S(2)}) copy-start(bf16[128,256]{1,0:T(8,128)(2,1)} %keys_ref.1) | copy-start | bytes 196612
  3.6 7.3 %copy-start.7 = (bf16[128,256]{1,0:T(8,128)(2,1)S(1)}, bf16[128,256]{1,0:T(8,128)(2,1)}, u32[]{:S(2)}) copy-start(bf16[128,256]{1,0:T(8,128)(2,1)} %values_ref.1) | copy-start | bytes 196612
  3.6 11.0 %collective-permute-start = (bf16[144,1024]{1,0:T(8,128)(2,1)}, bf16[144,1024]{1,0:T(8,128)(2,1)S(1)}, u32[]{:S(2)}, u32[]{:S(2)}) collective-permute-start(bf16[144,1024]{1,0:T(8,128)(2,1)} %first_state.1.refs_13_.refs_1_), channel_id=1, source_target_pairs={{0,4},{4,8},{8,12},{1,5},{5,9},{9,13},{2,6},{6,10},{10,14},{3,7},{... | collective-permute-start | bytes 884744 | tf_op jit(solution)/shard_map/ppermute | solution.py:605
  11.0 3.6 %copy-start.3 = (bf16[144,1024]{1,0:T(8,128)(2,1)S(1)}, bf16[144,1024]{1,0:T(8,128)(2,1)}, u32[]{:S(2)}) copy-start(bf16[144,1024]{1,0:T(8,128)(2,1)} %first_state.1.refs_13_.refs_1_) | copy-start | bytes 884740
  11.8 7.7 %collective-permute-start.3 = (bf16[128,512]{1,0:T(8,128)(2,1)S(1)}, bf16[128,512]{1,0:T(8,128)(2,1)S(1)}, u32[]{:S(2)}, u32[]{:S(2)}) collective-permute-start(bf16[128,512]{1,0:T(8,128)(2,1)S(1)} %get-tuple-element.47), channel_id=1, source_target_pairs={{0,4},{4,8},{8,12},{1,5},{5,9},{9,13},{2,6},{6,10},{10,14},{3,7},{... | collective-permute-start | bytes 393224 | tf_op jit(solution)/shard_map/ppermute | solution.py:605
  14.7 9.5 %collective-permute-start.1 = (bf16[128,1024]{1,0:T(8,128)(2,1)S(1)}, bf16[128,1024]{1,0:T(8,128)(2,1)S(1)}, u32[]{:S(2)}, u32[]{:S(2)}) collective-permute-start(bf16[128,1024]{1,0:T(8,128)(2,1)S(1)} %relay_slot2.1), channel_id=1, source_target_pairs={{0,4},{4,8},{8,12},{1,5},{5,9},{9,13},{2,6},{6,10},{10,14},{3,7},{... | collective-permute-start | bytes 786440 | tf_op jit(solution)/shard_map/ppermute | solution.py:605
  18.2 1.2 %copy-start = (f32[2048]{0:T(1024)S(1)}, f32[2048]{0:T(1024)}, u32[]{:S(2)}) copy-start(f32[2048]{0:T(1024)} %refs_3_.11) | copy-start | bytes 24580
  20.2 7.7 %collective-permute-start.4 = (bf16[128,512]{1,0:T(8,128)(2,1)S(1)}, bf16[128,512]{1,0:T(8,128)(2,1)S(1)}, u32[]{:S(2)}, u32[]{:S(2)}) collective-permute-start(bf16[128,512]{1,0:T(8,128)(2,1)S(1)} %get-tuple-element.55), channel_id=1, source_target_pairs={{4,8},{8,12},{5,9},{9,13},{6,10},{10,14},{7,11},{11,15},{20,24},{2... | collective-permute-start | bytes 393224 | tf_op jit(solution)/shard_map/ppermute | solution.py:605
  24.3 8.6 %collective-permute-start.2 = (bf16[128,1024]{1,0:T(8,128)(2,1)S(1)}, bf16[128,1024]{1,0:T(8,128)(2,1)S(1)}, u32[]{:S(2)}, u32[]{:S(2)}) collective-permute-start(bf16[128,1024]{1,0:T(8,128)(2,1)S(1)} %relay_slot3.1), channel_id=1, source_target_pairs={{4,8},{8,12},{5,9},{9,13},{6,10},{10,14},{7,11},{11,15},{20,24},{2... | collective-permute-start | bytes 786440 | tf_op jit(solution)/shard_map/ppermute | solution.py:605

commit v3 on v2

--- a/solution.py
+++ b/solution.py
@@ -112,7 +112,11 @@
     return conv(pad, raw.shape[0], weight, bias.reshape(1, -1), inside)
 
 
-def first_state_kernel(*refs):
+def first_state_kernel(count, *refs):
+    pl.when(lax.axis_index("seq") < count - 1)(functools.partial(first_state, *refs))
+
+
+def first_state(*refs):
     hbm_refs, out_hbm_ref = refs[:10], refs[10]
     vmem_refs = refs[11:21]
     x_edge_ref, bc_edge_ref, out_ref, b_pad_ref, pad_ref, in_sems, out_sems = refs[21:]
@@ -639,7 +643,7 @@
     tail_rows = EDGE * -(-4 * pieces // EDGE)
 
     (message,) = call(
-        first_state_kernel,
+        functools.partial(first_state_kernel, count),
         "first_state",
         [shape((STATE + tail_rows, per_group), BF16)],
         [x_raw, bc_raw, *(a if a.ndim > 1 else a[None] for a in params), doc_lens],

time: 34.3 us -> 33.7 us (0.983)
  starting transfers between devices: 14.6 us -> 10.9 us
  waiting for transfers between devices: 5.35 us -> 8.45 us
    ppermute x5, starting transfers between devices: 14.6 us -> 10.9 us  [onward(): lax.ppermute(value, 'seq', [(source, source + 1) for source in range(firs...]
    ppermute x5, waiting for transfers between devices: 5.35 us -> 8.45 us  [onward(): lax.ppermute(value, 'seq', [(source, source + 1) for source in range(firs...]
where the time goes in v3:
time: 33.7 us; the launch traced here: 33.5 us
  Pallas kernels  13 us (39%)
  starting transfers between devices  10.9 us (32%)
  waiting for transfers between devices  8.45 us (25%)
  between operations  0.99 us (3%)
    pallas_call x12, Pallas kernels, call(): pl.pallas_call(kernel, name=name, grid=(1,), out_shape=outs, in_specs=spe...  13 us
    ppermute x5, starting transfers between devices, onward(): lax.ppermute(value, 'seq', [(source, source + 1) for source in range(firs...  10.9 us
    ppermute x5, waiting for transfers between devices, onward(): lax.ppermute(value, 'seq', [(source, source + 1) for source in range(firs...  8.45 us
  transfers between devices with their start and end apart: 5, of which 3 were waited for; matrix products, arithmetic and copies ran while one was open for 0% of the time, Pallas kernels for 27%

profile of v3, /device:TPU:22, one launch (start us, length us, event | category | flops | bytes accessed | tf_op | source)
XLA Modules:
  0.0 33.5 jit_solution(8531805823149940760)
XLA Ops:
  0.6 0.0 copy-start.1
  0.6 0.0 copy-start.2
  0.7 0.0 copy-start.5
  0.7 0.0 copy-start.8
  0.7 0.0 copy-start.9
  0.7 0.0 copy-start.10
  0.7 0.0 copy-start.11
  0.8 2.9 %first_state.1.refs_13_.refs_1_ = bf16[144,1024]{1,0:T(8,128)(2,1)} custom-call(bf16[128,2048]{1,0:T(8,128)(2,1)} %refs_0_.4, bf16[128,512]{1,0:T(8,128)(2,1)} %refs_1_.3, f32[32,128]{1,0:T(8,128)} %bitcast.5, f32[4,2048]{1,0:T(4,128)} %refs_7_.3, f32[1,2048]{1,0:T(1,128)} %bitcast.7, f32[4,512]{1,0:T(4,128)} %refs_8_.3, f32[1,512]{1,0:T(1,128)} %bitcast.8, ...), custom_call_target="tpu_custom_call" | custom-call | flops 2000000000 | bytes 1018128 | tf_op jit(solution)/shard_map/first_state/pallas_call | solution.py:593
  3.6 0.0 copy-start.4
  3.6 0.0 copy-start.6
  3.6 0.0 copy-start.7
  3.7 2.1 %collective-permute-start = (bf16[144,1024]{1,0:T(8,128)(2,1)}, bf16[144,1024]{1,0:T(8,128)(2,1)S(1)}, u32[]{:S(2)}, u32[]{:S(2)}) collective-permute-start(bf16[144,1024]{1,0:T(8,128)(2,1)} %first_state.1.refs_13_.refs_1_), channel_id=1, source_target_pairs={{0,4},{4,8},{8,12},{1,5},{5,9},{9,13},{2,6},{6,10},{10,14},{3,7},{... | collective-permute-start | bytes 884744 | tf_op jit(solution)/shard_map/ppermute | solution.py:609
  5.8 3.6 %prepare.1 = (bf16[128,2048]{1,0:T(8,128)(2,1)}, bf16[128,512]{1,0:T(8,128)(2,1)S(1)}, f32[8,2560]{1,0:T(8,128)S(1)}, f32[8,2048]{1,0:T(8,128)S(1)}, f32[8,2048]...) custom-call(bf16[128,2048]{1,0:T(8,128)(2,1)S(1)} %copy-done.1, ...), custom_call_target="tpu_custom_call" | custom-call | flops 2000000000 | bytes 5728656 | tf_op jit(solution)/shard_map/prepare/pallas_call | solution.py:593
  9.4 0.8 %attend_own.1 = (f32[128,1024]{1,0:T(8,128)S(1)}, f32[128,1024]{1,0:T(8,128)S(1)}, f32[128,1024]{1,0:T(8,128)S(1)}, bf16[128,512]{1,0:T(8,128)(2,1)S(1)}) custom-call(bf16[128,1024]{1,0:T(8,128)(2,1)S(1)} %copy-done.4, bf16[128,256]{1,0:T(8,128)(2,1)S(1)} %copy-done.6, bf16[128,256]{1,0:T(8,128)(2,1)S(1)} %copy-done.7, ...), custom_call_target="tpu_custom_call" | custom-call | flops 2000000000 | bytes 2162688 | tf_op jit(solution)/shard_map/attend_own/pallas_call | solution.py:593
  10.2 1.9 %collective-permute-start.3 = (bf16[128,512]{1,0:T(8,128)(2,1)S(1)}, bf16[128,512]{1,0:T(8,128)(2,1)S(1)}, u32[]{:S(2)}, u32[]{:S(2)}) collective-permute-start(bf16[128,512]{1,0:T(8,128)(2,1)S(1)} %get-tuple-element.47), channel_id=1, source_target_pairs={{0,4},{4,8},{8,12},{1,5},{5,9},{9,13},{2,6},{6,10},{10,14},{3,7},{... | collective-permute-start | bytes 393224 | tf_op jit(solution)/shard_map/ppermute | solution.py:609
  12.1 2.5 %collective-permute-done.refs_0_.refs_5_ = bf16[144,1024]{1,0:T(8,128)(2,1)S(1)} collective-permute-done((bf16[144,1024]{1,0:T(8,128)(2,1)}, bf16[144,1024]{1,0:T(8,128)(2,1)S(1)}, u32[]{:S(2)}, u32[]{:S(2)}) %collective-permute-start) | collective-permute-done | bytes 294944 | tf_op jit(solution)/shard_map/ppermute | solution.py:609
  14.7 0.1 relay_slot2.1
  14.7 2.2 %collective-permute-start.1 = (bf16[128,1024]{1,0:T(8,128)(2,1)S(1)}, bf16[128,1024]{1,0:T(8,128)(2,1)S(1)}, u32[]{:S(2)}, u32[]{:S(2)}) collective-permute-start(bf16[128,1024]{1,0:T(8,128)(2,1)S(1)} %relay_slot2.1), channel_id=1, source_target_pairs={{0,4},{4,8},{8,12},{1,5},{5,9},{9,13},{2,6},{6,10},{10,14},{3,7},{... | collective-permute-start | bytes 786440 | tf_op jit(solution)/shard_map/ppermute | solution.py:609
  17.0 0.0 copy-start
  17.0 1.2 %first_rows.1 = (f32[128,2048]{1,0:T(8,128)S(1)}, bf16[128,256]{1,0:T(8,128)(2,1)S(1)}, bf16[128,1024]{1,0:T(8,128)(2,1)}, bf16[128,1024]{1,0:T(8,128)(2,1)S(1)}) custom-call(bf16[144,1024]{1,0:T(8,128)(2,1)S(1)} %collective-permute-done.refs_0_.refs_5_, f32[8,2560]{1,0:T(8,128)S(1)} %get-tuple-element.29.refs_1_.refs_2_, ...), custom_call_target="tpu_custom_call" | custom-call | flops 2000000000 | bytes 5095424 | tf_op jit(solution)/shard_map/first_rows/pallas_call | solution.py:593
  18.2 0.0 collective-permute-done.3.before_ref
  18.2 0.8 %attend_near.1 = (f32[128,1024]{1,0:T(8,128)S(1)}, f32[128,1024]{1,0:T(8,128)S(1)}, f32[128,1024]{1,0:T(8,128)S(1)}, bf16[128,512]{1,0:T(8,128)(2,1)S(1)}) custom-call(bf16[128,1024]{1,0:T(8,128)(2,1)S(1)} %copy-done.4, bf16[128,512]{1,0:T(8,128)(2,1)S(1)} %collective-permute-done.3.before_ref, s32[128,128]{1,0:T(8,128)S(1)} %get-tuple-element.35.refs_9_.begin_ref.refs_1_, ...), custom_call_target="tpu_custom_call" | custom-call | flops 2000000000 | bytes 3739648 | tf_op jit(solution)/shard_map/attend_near/pallas_call | solution.py:593
  19.0 1.9 %collective-permute-start.4 = (bf16[128,512]{1,0:T(8,128)(2,1)S(1)}, bf16[128,512]{1,0:T(8,128)(2,1)S(1)}, u32[]{:S(2)}, u32[]{:S(2)}) collective-permute-start(bf16[128,512]{1,0:T(8,128)(2,1)S(1)} %get-tuple-element.55), channel_id=1, source_target_pairs={{4,8},{8,12},{5,9},{9,13},{6,10},{10,14},{7,11},{11,15},{20,24},{2... | collective-permute-start | bytes 393224 | tf_op jit(solution)/shard_map/ppermute | solution.py:609
  20.9 3.1 %collective-permute-done.1.refs_0_.refs_6_.refs_5_ = bf16[128,1024]{1,0:T(8,128)(2,1)S(1)} collective-permute-done((bf16[128,1024]{1,0:T(8,128)(2,1)S(1)}, bf16[128,1024]{1,0:T(8,128)(2,1)S(1)}, u32[]{:S(2)}, u32[]{:S(2)}) %collective-permute-start.1) | collective-permute-done | bytes 262176 | tf_op jit(solution)/shard_map/ppermute | solution.py:609
  24.0 0.1 relay_slot3.1
  24.1 2.8 %collective-permute-start.2 = (bf16[128,1024]{1,0:T(8,128)(2,1)S(1)}, bf16[128,1024]{1,0:T(8,128)(2,1)S(1)}, u32[]{:S(2)}, u32[]{:S(2)}) collective-permute-start(bf16[128,1024]{1,0:T(8,128)(2,1)S(1)} %relay_slot3.1), channel_id=1, source_target_pairs={{4,8},{8,12},{5,9},{9,13},{6,10},{10,14},{7,11},{11,15},{20,24},{2... | collective-permute-start | bytes 786440 | tf_op jit(solution)/shard_map/ppermute | solution.py:609
  27.0 0.0 collective-permute-done.4.refs_5_
  27.0 1.5 %attend_far.1 = bf16[128,1024]{1,0:T(8,128)(2,1)} custom-call(bf16[128,1024]{1,0:T(8,128)(2,1)S(1)} %copy-done.4, s32[128,128]{1,0:T(8,128)S(1)} %get-tuple-element.35.refs_9_.begin_ref.refs_1_, f32[128,1024]{1,0:T(8,128)S(1)} %get-tuple-element.52.refs_2_, f32[128,1024]{1,0:T(8,128)S(1)} %get-tuple-element.53.refs_3_, ...), custom_call_target="tpu_custom_call" | custom-call | flops 2000000000 | bytes 2293760 | tf_op jit(solution)/shard_map/attend_far/pallas_call | solution.py:593
  28.5 1.1 %norm_part0_rest.1.refs_6_ = bf16[128,2048]{1,0:T(8,128)(2,1)} custom-call(f32[128,2048]{1,0:T(8,128)S(1)} %get-tuple-element.40.refs_0_, f32[128,2048]{1,0:T(8,128)S(1)} %get-tuple-element.41.refs_1_, bf16[128,256]{1,0:T(8,128)(2,1)S(1)} %get-tuple-element.42.refs_2_, f32[2048]{0:T(1024)S(1)} %copy-done, ...), custom_call_target="tpu_custom_call", output_to_operand_aliasing={{}: (7, {})} | custom-call | flops 1000000000 | bytes 3792896 | tf_op jit(solution)/shard_map/norm_part0_rest/pallas_call | solution.py:593
  29.6 0.1 norm_part1_first.1.refs_6_
  29.6 2.8 %collective-permute-done.2.refs_5_ = bf16[128,1024]{1,0:T(8,128)(2,1)S(1)} collective-permute-done((bf16[128,1024]{1,0:T(8,128)(2,1)S(1)}, bf16[128,1024]{1,0:T(8,128)(2,1)S(1)}, u32[]{:S(2)}, u32[]{:S(2)}) %collective-permute-start.2) | collective-permute-done | bytes 262176 | tf_op jit(solution)/shard_map/ppermute | solution.py:609
  32.4 1.1 %norm_part1_later.1 = bf16[128,2048]{1,0:T(8,128)(2,1)} custom-call(f32[128,2048]{1,0:T(8,128)S(1)} %get-tuple-element.40.refs_0_, f32[128,2048]{1,0:T(8,128)S(1)} %get-tuple-element.41.refs_1_, bf16[128,256]{1,0:T(8,128)(2,1)S(1)} %get-tuple-element.42.refs_2_, f32[2048]{0:T(1024)S(1)} %copy-done, ...), custom_call_target="tpu_custom_call", output_to_operand_aliasing={{}: (6, {})} | custom-call | flops 1000000000 | bytes 3497984 | tf_op jit(solution)/shard_map/norm_part1_later/pallas_call | solution.py:593
  (24 shorter events, 0.1 us)
Async XLA Ops:
  0.6 5.1 %copy-start.1 = (bf16[128,2048]{1,0:T(8,128)(2,1)S(1)}, bf16[128,2048]{1,0:T(8,128)(2,1)}, u32[]{:S(2)}) copy-start(bf16[128,2048]{1,0:T(8,128)(2,1)} %refs_0_.4) | copy-start | bytes 1572868
  0.6 5.1 %copy-start.2 = (bf16[128,2048]{1,0:T(8,128)(2,1)S(1)}, bf16[128,2048]{1,0:T(8,128)(2,1)}, u32[]{:S(2)}) copy-start(bf16[128,2048]{1,0:T(8,128)(2,1)} %refs_11_.1) | copy-start | bytes 1572868
  0.7 5.1 %copy-start.5 = (bf16[128,512]{1,0:T(8,128)(2,1)S(1)}, bf16[128,512]{1,0:T(8,128)(2,1)}, u32[]{:S(2)}) copy-start(bf16[128,512]{1,0:T(8,128)(2,1)} %refs_1_.3) | copy-start | bytes 393220
  0.7 5.1 %copy-start.8 = (f32[4,2048]{1,0:T(4,128)S(1)}, f32[4,2048]{1,0:T(4,128)}, u32[]{:S(2)}) copy-start(f32[4,2048]{1,0:T(4,128)} %refs_7_.3) | copy-start | bytes 98308
  0.7 5.1 %copy-start.9 = (f32[128,32]{0,1:T(8,128)S(1)}, f32[128,32]{0,1:T(8,128)}, u32[]{:S(2)}) copy-start(f32[128,32]{0,1:T(8,128)} %param.19) | copy-start | bytes 49156
  0.7 5.1 %copy-start.10 = (f32[2048]{0:T(1024)S(1)}, f32[2048]{0:T(1024)}, u32[]{:S(2)}) copy-start(f32[2048]{0:T(1024)} %refs_4_.2) | copy-start | bytes 24580
  0.7 5.1 %copy-start.11 = (f32[4,512]{1,0:T(4,128)S(1)}, f32[4,512]{1,0:T(4,128)}, u32[]{:S(2)}) copy-start(f32[4,512]{1,0:T(4,128)} %refs_8_.3) | copy-start | bytes 24580
  0.7 5.1 %copy-start.12 = (f32[512]{0:T(512)S(1)}, f32[512]{0:T(512)}, u32[]{:S(2)}) copy-start(f32[512]{0:T(512)} %refs_6_.1) | copy-start | bytes 6148
  0.7 5.1 %copy-start.13 = (f32[32]{0:T(128)S(1)}, f32[32]{0:T(128)}, u32[]{:S(2)}) copy-start(f32[32]{0:T(128)} %refs_7_.2) | copy-start | bytes 388
  0.7 5.1 %copy-start.14 = (f32[32]{0:T(128)S(1)}, f32[32]{0:T(128)}, u32[]{:S(2)}) copy-start(f32[32]{0:T(128)} %refs_8_.2) | copy-start | bytes 388
  0.7 5.1 %copy-start.15 = (s32[4]{0:T(128)S(1)}, s32[4]{0:T(128)}, u32[]{:S(2)}) copy-start(s32[4]{0:T(128)} %refs_10_.1) | copy-start | bytes 52
  0.7 5.1 %copy-start.16 = (f32[32]{0:T(128)S(1)}, f32[32]{0:T(128)}, u32[]{:S(2)}) copy-start(f32[32]{0:T(128)} %refs_9_.3) | copy-start | bytes 388
  3.6 5.8 %copy-start.4 = (bf16[128,1024]{1,0:T(8,128)(2,1)S(1)}, bf16[128,1024]{1,0:T(8,128)(2,1)}, u32[]{:S(2)}) copy-start(bf16[128,1024]{1,0:T(8,128)(2,1)} %refs_0_.5) | copy-start | bytes 786436
  3.6 5.8 %copy-start.6 = (bf16[128,256]{1,0:T(8,128)(2,1)S(1)}, bf16[128,256]{1,0:T(8,128)(2,1)}, u32[]{:S(2)}) copy-start(bf16[128,256]{1,0:T(8,128)(2,1)} %keys_ref.1) | copy-start | bytes 196612
  3.6 5.8 %copy-start.7 = (bf16[128,256]{1,0:T(8,128)(2,1)S(1)}, bf16[128,256]{1,0:T(8,128)(2,1)}, u32[]{:S(2)}) copy-start(bf16[128,256]{1,0:T(8,128)(2,1)} %values_ref.1) | copy-start | bytes 196612
  3.7 11.0 %collective-permute-start = (bf16[144,1024]{1,0:T(8,128)(2,1)}, bf16[144,1024]{1,0:T(8,128)(2,1)S(1)}, u32[]{:S(2)}, u32[]{:S(2)}) collective-permute-start(bf16[144,1024]{1,0:T(8,128)(2,1)} %first_state.1.refs_13_.refs_1_), channel_id=1, source_target_pairs={{0,4},{4,8},{8,12},{1,5},{5,9},{9,13},{2,6},{6,10},{10,14},{3,7},{... | collective-permute-start | bytes 884744 | tf_op jit(solution)/shard_map/ppermute | solution.py:609
  9.4 5.3 %copy-start.3 = (bf16[144,1024]{1,0:T(8,128)(2,1)S(1)}, bf16[144,1024]{1,0:T(8,128)(2,1)}, u32[]{:S(2)}) copy-start(bf16[144,1024]{1,0:T(8,128)(2,1)} %first_state.1.refs_13_.refs_1_) | copy-start | bytes 884740
  10.2 8.0 %collective-permute-start.3 = (bf16[128,512]{1,0:T(8,128)(2,1)S(1)}, bf16[128,512]{1,0:T(8,128)(2,1)S(1)}, u32[]{:S(2)}, u32[]{:S(2)}) collective-permute-start(bf16[128,512]{1,0:T(8,128)(2,1)S(1)} %get-tuple-element.47), channel_id=1, source_target_pairs={{0,4},{4,8},{8,12},{1,5},{5,9},{9,13},{2,6},{6,10},{10,14},{3,7},{... | collective-permute-start | bytes 393224 | tf_op jit(solution)/shard_map/ppermute | solution.py:609
  14.7 9.3 %collective-permute-start.1 = (bf16[128,1024]{1,0:T(8,128)(2,1)S(1)}, bf16[128,1024]{1,0:T(8,128)(2,1)S(1)}, u32[]{:S(2)}, u32[]{:S(2)}) collective-permute-start(bf16[128,1024]{1,0:T(8,128)(2,1)S(1)} %relay_slot2.1), channel_id=1, source_target_pairs={{0,4},{4,8},{8,12},{1,5},{5,9},{9,13},{2,6},{6,10},{10,14},{3,7},{... | collective-permute-start | bytes 786440 | tf_op jit(solution)/shard_map/ppermute | solution.py:609
  17.0 1.2 %copy-start = (f32[2048]{0:T(1024)S(1)}, f32[2048]{0:T(1024)}, u32[]{:S(2)}) copy-start(f32[2048]{0:T(1024)} %refs_3_.11) | copy-start | bytes 24580
  19.0 8.0 %collective-permute-start.4 = (bf16[128,512]{1,0:T(8,128)(2,1)S(1)}, bf16[128,512]{1,0:T(8,128)(2,1)S(1)}, u32[]{:S(2)}, u32[]{:S(2)}) collective-permute-start(bf16[128,512]{1,0:T(8,128)(2,1)S(1)} %get-tuple-element.55), channel_id=1, source_target_pairs={{4,8},{8,12},{5,9},{9,13},{6,10},{10,14},{7,11},{11,15},{20,24},{2... | collective-permute-start | bytes 393224 | tf_op jit(solution)/shard_map/ppermute | solution.py:609
  24.1 8.3 %collective-permute-start.2 = (bf16[128,1024]{1,0:T(8,128)(2,1)S(1)}, bf16[128,1024]{1,0:T(8,128)(2,1)S(1)}, u32[]{:S(2)}, u32[]{:S(2)}) collective-permute-start(bf16[128,1024]{1,0:T(8,128)(2,1)S(1)} %relay_slot3.1), channel_id=1, source_target_pairs={{4,8},{8,12},{5,9},{9,13},{6,10},{10,14},{7,11},{11,15},{20,24},{2... | collective-permute-start | bytes 786440 | tf_op jit(solution)/shard_map/ppermute | solution.py:609
